TPU v7x, 32 devices: a whole 2x2x4 slice. The times are simulated.
32 devices in a mesh: dp: 16 (over z, x, core), expert: 2 (over y).
Axes of the slice: x: 2, y: 2, z: 4, core: 2. Of those that a mesh axis runs over, the one named last changes fastest.
Arguments:
- grad_out: bfloat16 [8192, 1024], P(('dp', 'expert')), may hold values from -1 to 1
- routes: int32 [8192, 6], P(('dp', 'expert')), may hold values from 0 to 63, all different within a row; in each aligned block of 256 rows (0 to 255, 256 to 511, ...) at most 48 rows name the same one
- route_weight: float32 [8192, 6], P(('dp', 'expert')), may hold values from 0.05 to 0.35
- example_ids: int32 [16, 512], P('dp', 'expert'), may hold values from 0 to 7, never falling along the last dimension, each value on 1 to 128 neighbouring positions
- example_weight: float32 [16, 8], P('dp'), may hold values from 0.5 to 50
- hidden: bfloat16 [16, 2, 2, 48, 704], P('dp', 'expert'), may hold values from -6 to 6
Outputs:
- expert_grads: float32 [704, 2, 1024], P('dp', 'expert')
Inputs may be any that keep to these rules, and one draw needn't show every extreme that they name: `routes`: each row names 6 different experts; in the rows of one device no expert is named more than 48 times, a bound that some block reaches. `example_ids`: along a data group's tokens the numbers never fall; each of the 8 examples has from 1 to a quarter of 512 tokens, one exactly that many.
All inputs are finite; a program needn't handle non-finite values.
Results may differ from a plain program's by a relative error of at most 0.0011.
Values may be sent and summed in bfloat16 or wider, within the bound.
No kernel may reach another device: no remote copies, remote signals or barrier semaphores. Data moves between devices by JAX's collectives and lax.ppermute only.
A program may use at most 64 MiB of HBM per device.

v0:
```python
import jax
import jax.numpy as jnp
from jax import lax
from jax.sharding import PartitionSpec as P

FF_WIN = 704
D_WIN = 1024
EXAMPLES = 8


def slot_layout(block_routes, expert_list, capacity):
    matches = (block_routes[..., None] == expert_list).astype(jnp.float32)
    routed = jnp.sum(matches, axis=-2)
    ranking = jnp.cumsum(routed, axis=-2) - routed
    slot_index = jnp.arange(capacity).astype(jnp.float32)
    placed = routed[..., None] * (ranking[..., None] == slot_index).astype(jnp.float32)
    return (matches, placed)


def shards(grad_out, routes, route_weight, example_ids, example_weight, hidden):
    highest = lax.Precision.HIGHEST
    sources = lax.axis_size("expert")
    device = lax.axis_index("expert")
    tokens_here = grad_out.shape[0]
    top_count = routes.shape[1]
    local_experts = hidden.shape[1]
    capacity = hidden.shape[3]
    slot_total = sources * capacity
    in_flight = jnp.arange(sources * local_experts, dtype=jnp.int32)
    example_index = jnp.arange(EXAMPLES, dtype=jnp.int32)
    own_ids = example_ids.reshape(tokens_here)
    own_members = (own_ids[:, None] == example_index).astype(jnp.float32)
    token_weight = jnp.sum(own_members * example_weight[0], axis=1)
    matches, placed = slot_layout(routes, in_flight, capacity)
    token_scale = jnp.sum(matches * route_weight[:, :, None], axis=1) * token_weight[:, None]
    dispatch = placed.astype(jnp.bfloat16)
    slot_rows = jnp.einsum("tec,td->ecd", dispatch, grad_out, preferred_element_type=jnp.float32)
    slot_scale = jnp.sum(placed * token_scale[:, :, None], axis=0)
    outgoing = (
        (slot_rows * slot_scale[:, :, None])
        .astype(jnp.bfloat16)
        .reshape(sources, local_experts, capacity, D_WIN)
    )
    incoming = lax.all_to_all(outgoing, "expert", split_axis=0, concat_axis=0, tiled=True)
    group_routes, group_ids = (
        lax.all_gather(routes, "expert", axis=0, tiled=True),
        lax.all_gather(own_ids, "expert", axis=0, tiled=True),
    )
    own_experts = device * local_experts + jnp.arange(local_experts, dtype=jnp.int32)
    unused_matches, group_placed = slot_layout(
        group_routes.reshape(sources, tokens_here, top_count), own_experts, capacity
    )
    group_members = (group_ids.reshape(sources, tokens_here)[:, :, None] == example_index).astype(
        jnp.float32
    )
    member = jnp.einsum("stjc,stx->jscx", group_placed, group_members, precision=highest).reshape(
        local_experts, slot_total, EXAMPLES
    )
    acts_slots = hidden[0].reshape(local_experts, slot_total, FF_WIN)
    cot_slots = jnp.transpose(incoming, (1, 0, 2, 3)).reshape(local_experts, slot_total, D_WIN)
    gram_left = jnp.einsum(
        "jif,jkf->jik", acts_slots, acts_slots, preferred_element_type=jnp.float32
    )
    gram_right = jnp.einsum(
        "jid,jkd->jik", cot_slots, cot_slots, preferred_element_type=jnp.float32
    )
    spread = jnp.einsum("jik,jkx->jix", gram_left * gram_right, member, precision=highest)
    squares = jnp.sum(spread * member, axis=(0, 1))
    total_squares = lax.psum(squares, "expert")
    clip_factor = 1.0 / jnp.maximum(jnp.sqrt(total_squares / (FF_WIN * D_WIN)), 1.0)
    slot_weight = jnp.sum(member * clip_factor, axis=2) / EXAMPLES
    scaled = (slot_weight[:, :, None] * cot_slots.astype(jnp.float32)).astype(jnp.bfloat16)
    return lax.psum_scatter(
        jnp.einsum("jif,jid->fjd", acts_slots, scaled, preferred_element_type=jnp.float32),
        "dp",
        scatter_dimension=0,
        tiled=True,
    )


def solution(mesh):
    placed = (
        P(("dp", "expert"), None),
        P(("dp", "expert"), None),
        P(("dp", "expert"), None),
        P("dp", "expert"),
        P("dp", None),
        P("dp", "expert", None, None, None),
    )
    return jax.shard_map(
        shards, mesh=mesh, in_specs=placed, out_specs=P("dp", "expert", None), check_vma=False
    )
```

profile of v0, /device:TPU:0, one launch (start us, length us, event | category | flops | bytes accessed | tf_op | source)
XLA Modules:
  0.0 152.2 jit_solution(8960468166035746879)
XLA Ops:
  6.5 0.0 copy-start
  6.5 0.8 convert_reduce_fusion.1
  7.4 0.6 reduce-window.16
  8.0 0.2 slice_reduce_fusion
  8.1 0.2 reduce-window.19
  8.3 0.1 add_bitcast_fusion
  8.4 0.8 select_reduce_fusion.1
  9.2 0.2 fusion.8
  9.3 0.0 copy-done
  9.3 0.9 fusion.1
  10.3 4.2 %all-to-all-start = ((bf16[2,1,48,1024]{3,2,1,0:T(8,128)(2,1)}), bf16[2,1,48,1024]{3,2,1,0:T(8,128)(2,1)S(1)}, u32[]{:S(2)}, u32[]{:S(2)}) async-start(bf16[2,1,48,1024]{3,2,1,0:T(8,128)(2,1)} %fusion.1), calls=%async_computation | async-start | bytes 393216 | tf_op jit(solution)/shard_map/all_to_all | solution.py:44
  14.5 0.0 all-reduce.3.cloned.1.call-start
  14.5 5.4 %all_gather.7 = s32[512,6]{0,1:T(8,128)S(1)} all-gather(s32[256,6]{0,1:T(8,128)} %param.7), channel_id=1, replica_groups=mesh['dp'=16,'expert'=2] {'expert'}, dimensions={0}, use_global_device_ids=true | all-gather | bytes 18432 | tf_op jit(solution)/shard_map/all_gather | solution.py:46
  19.9 4.4 %all-gather = s32[1,512]{1,0:T(1,128)S(1)} all-gather(s32[1,256]{1,0:T(1,128)} %param.9), channel_id=2, replica_groups=mesh['dp'=16,'expert'=2] {'expert'}, dimensions={1}, use_global_device_ids=true | all-gather | bytes 3072 | tf_op jit(solution)/shard_map/all_gather | solution.py:47
  24.4 0.6 reduce-window.14
  25.0 0.2 slice_reduce_fusion.1
  25.1 0.2 reduce-window.15
  25.3 0.1 broadcast_bitcast_fusion
  25.4 0.5 broadcast.133
  25.9 0.7 reduce.12
  26.6 0.2 convolution_bitcast_fusion.1
  26.8 0.1 reshape.237
  26.9 0.0 all-to-all-done
  26.9 0.2 fusion.24
  27.1 1.2 convolution_multiply_fusion.1
  28.3 0.3 fusion.2
  28.6 4.9 %psum.7 = f32[8]{0:T(128)S(1)} all-reduce(f32[8]{0:T(128)S(1)} %fusion.2), channel_id=1, replica_groups=mesh['dp'=16,'expert'=2] {'expert'}, use_global_device_ids=true, to_apply=%region_10.11 | all-reduce | flops 8 | bytes 64 | tf_op jit(solution)/shard_map/psum | solution.py:69
  33.6 0.1 multiply_reduce_fusion
  33.7 0.1 div.18
  33.8 1.5 %convolution_bitcast_fusion = f32[704,1,1024]{2,0,1:T(8,128)S(1)} fusion(bf16[96,704]{1,0:T(8,128)(2,1)} %bitcast.63, bf16[1,96,1,1,1,1,1024]{6,1,5,4,3,2,0:T(8,128)(2,1)S(1)} %bitcast.61, f32[96]{0:T(128)S(1)} %div.18), kind=kOutput, calls=%fused_computation | convolution fusion | flops 138706944 | bytes 3215744 | tf_op jit(solution)/shard_map/jif,jid->fjd/dot_general | solution.py:74
  35.3 4.6 %copy.21 = f32[704,1,1024]{2,1,0:T(1,128)} copy(f32[704,1,1024]{2,0,1:T(8,128)S(1)} %convolution_bitcast_fusion) | data formatting | bytes 5767168 | tf_op jit(solution)/shard_map/jif,jid->fjd/transpose | solution.py:74
  39.9 0.0 copy-start.1
  39.9 0.0 all-reduce.3.cloned.1.call-update
  39.9 0.6 copy-done.1
  40.5 0.6 dynamic-slice
  41.8 101.9 %all-reduce.3.cloned.1.call-done = f32[704,1,1024]{2,1,0:T(1,128)} async-done(((f32[704,1,1024]{2,1,0:T(1,128)}), f32[704,1,1024]{2,1,0:T(1,128)}) %all-reduce.3.cloned.1.call-update) | async-done | bytes 2883600
  143.7 1.6 %constant_dynamic-slice_fusion = f32[44,1,1024]{2,1,0:T(1,128)} fusion(f32[704,1,1024]{2,1,0:T(1,128)} %all-reduce.3.cloned.1.call-done, u32[]{:T(128)S(6)} %multiply.10), kind=kLoop, calls=%fused_computation.45 | loop fusion | bytes 360452
  (11 shorter events, 0.1 us)
Async XLA Ops:
  6.5 2.8 %copy-start = (bf16[256,1024]{1,0:T(8,128)(2,1)S(1)}, bf16[256,1024]{1,0:T(8,128)(2,1)}, u32[]{:S(2)}) copy-start(bf16[256,1024]{1,0:T(8,128)(2,1)} %param.6) | copy-start | bytes 1572868
  10.3 16.6 %all-to-all-start = ((bf16[2,1,48,1024]{3,2,1,0:T(8,128)(2,1)}), bf16[2,1,48,1024]{3,2,1,0:T(8,128)(2,1)S(1)}, u32[]{:S(2)}, u32[]{:S(2)}) async-start(bf16[2,1,48,1024]{3,2,1,0:T(8,128)(2,1)} %fusion.1), calls=%async_computation | async-start | bytes 393216 | tf_op jit(solution)/shard_map/all_to_all | solution.py:44
  14.5 129.2 %all-reduce.3.cloned.1.call-start = ((), (), s32[]{:S(2)}) async-start(), calls=%async_computation.1 | async-start | bytes 5767168
  39.9 0.7 copy-start.1
Sparse Core Ops, SparseCore 0:
  40.0 103.6 all-reduce.2
where the time goes:
time: 153 us; the launch traced here: 152 us
  waiting for transfers between devices  102 us (67%)
  blocking collectives  14.8 us (10%)
  between operations  14.1 us (9%)
  local copies, waits for them, and re-layouts  8.53 us (6%)
  matrix products  4.4 us (3%)
  starting transfers between devices  4.24 us (3%)
  other arithmetic  4.2 us (3%)
    unnamed x2, waiting for transfers between devices  102 us
    all_gather x1, blocking collectives, shards(): lax.all_gather(routes, 'expert', axis=0, tiled=True)  5.37 us
    psum x1, blocking collectives, shards(): total_squares = lax.psum(squares, 'expert')  4.94 us
    transpose x1, local copies, waits for them, and re-layouts, shards(): jnp.einsum('jif,jid->fjd', acts_slots, scaled, preferred_element_type=jnp...  4.58 us
    all_gather x1, blocking collectives, shards(): lax.all_gather(own_ids, 'expert', axis=0, tiled=True)  4.45 us
    all_to_all x1, starting transfers between devices, shards(): lax.all_to_all(outgoing, 'expert', split_axis=0, concat_axis=0, tiled=True)  4.23 us
  transfers between devices with their start and end apart: 2, of which 1 were waited for; matrix products, arithmetic and copies ran while one was open for 2% of the time, Pallas kernels for 0%

commit v1 on v0

v1 whole, which is shorter than its diff:
```python
import jax
import jax.numpy as jnp
from jax import lax
from jax.sharding import PartitionSpec as P

EXAMPLES = 8


def shards(grad_out, routes, route_weight, example_ids, example_weight, hidden):
    sources = lax.axis_size("expert")
    me = lax.axis_index("expert")
    n_dp = lax.axis_size("dp")
    rank = lax.axis_index("dp")
    far = 4
    near = n_dp // far
    tokens = grad_out.shape[0]
    width = grad_out.shape[1]
    cap = hidden.shape[3]
    ff = hidden.shape[4]
    rows = ff // n_dp
    pad_rows = -(-rows // 16) * 16
    ids = example_ids.reshape(tokens)
    example_index = jnp.arange(EXAMPLES, dtype=jnp.int32)
    experts = jnp.arange(sources, dtype=jnp.int32)

    routes_t = routes.T
    hits = (routes_t[None] == experts[:, None, None]).astype(jnp.float32)
    routed = jnp.sum(hits, axis=1)
    token_weight = jnp.sum(
        jnp.where(ids[None, :] == example_index[:, None], example_weight[0][:, None], 0.0), axis=0
    )
    scale = jnp.sum(hits * route_weight.T[None], axis=1) * token_weight[None]
    order = jnp.arange(tokens)
    before = (order[:, None] < order[None, :]).astype(jnp.bfloat16)
    ranking = jnp.dot(routed.astype(jnp.bfloat16), before, preferred_element_type=jnp.float32)
    slot = jnp.arange(cap).astype(jnp.float32)
    placed = jnp.where(ranking[:, None, :] == slot[None, :, None], routed[:, None, :], 0.0)
    slot_scale = jnp.sum(placed * scale[:, None, :], axis=2)
    slot_code = jnp.sum(placed * (ids + 1).astype(jnp.float32)[None, None, :], axis=2)
    slot_rows = jnp.einsum(
        "ect,td->ecd", placed.astype(jnp.bfloat16), grad_out, preferred_element_type=jnp.float32
    )
    outgoing = (slot_rows * slot_scale[:, :, None]).astype(jnp.bfloat16)

    own_rows = lax.dynamic_index_in_dim(outgoing, me, 0, keepdims=False)
    own_code = lax.dynamic_index_in_dim(slot_code, me, 0, keepdims=False)
    rest_rows, codes = [], [own_code]
    acts = [lax.dynamic_index_in_dim(hidden[0, 0], me, 0, keepdims=False)]
    for k in range(1, sources):
        there = (me - k + sources) % sources
        pairs = [(s, (s - k) % sources) for s in range(sources)]
        send = lax.dynamic_index_in_dim(outgoing, there, 0, keepdims=False)
        send_code = lax.dynamic_index_in_dim(slot_code, there, 0, keepdims=False)
        rest_rows.append(lax.ppermute(send, "expert", pairs))
        codes.append(lax.ppermute(send_code, "expert", pairs))
        acts.append(lax.dynamic_index_in_dim(hidden[0, 0], (me + k) % sources, 0, keepdims=False))
    rest = jnp.concatenate(rest_rows, axis=0)
    code = jnp.concatenate(codes, axis=0)
    acts = jnp.concatenate(acts, axis=0)

    mine = rank // near

    def over_far(array, k):
        pairs = [
            (a * near + b, ((a + k) % far) * near + b) for a in range(far) for b in range(near)
        ]
        return lax.ppermute(array, "dp", pairs)

    cuts = acts.reshape(sources * cap, far, near, rows).transpose(1, 2, 3, 0)
    cuts = jnp.pad(cuts, ((0, 0), (0, 0), (0, pad_rows - rows), (0, 0)))
    cuts = cuts.reshape(far, near * pad_rows, sources * cap)
    own_far, rest_far, cut_far = [own_rows], [rest], []
    for k in range(far):
        cut = lax.dynamic_index_in_dim(cuts, (mine + k) % far, 0, keepdims=False)
        cut_far.append(cut if k == 0 else over_far(cut, k))
    for k in range(1, far):
        own_far.append(over_far(own_rows, k))
    for k in range(1, far):
        rest_far.append(over_far(rest, k))

    cot = jnp.concatenate([own_rows, rest], axis=0)
    left = lax.dot_general(
        acts, acts, (((1,), (1,)), ((), ())), preferred_element_type=jnp.float32
    )
    right = lax.dot_general(cot, cot, (((1,), (1,)), ((), ())), preferred_element_type=jnp.float32)
    alike = code[:, None] == code[None, :]
    per_slot = jnp.sum(jnp.where(alike, left * right, 0.0), axis=1)
    member = (code[:, None] == (example_index + 1).astype(jnp.float32)[None]).astype(jnp.float32)
    squares = jnp.sum(per_slot[:, None] * member, axis=0)
    total = squares
    for k in range(1, sources):
        total = total + lax.ppermute(
            squares, "expert", [(s, (s - k) % sources) for s in range(sources)]
        )
    clip = 1.0 / jnp.maximum(jnp.sqrt(total / (ff * width)), 1.0)
    weight = jnp.sum(member * clip[None], axis=1) / EXAMPLES
    weights = [weight] + [over_far(weight, k) for k in range(1, far)]

    part = jnp.zeros((near * pad_rows, width), jnp.float32)
    for k in range(far):
        rows_k = jnp.concatenate([own_far[k], rest_far[k]], axis=0)
        scaled = (weights[k][:, None] * rows_k.astype(jnp.float32)).astype(jnp.bfloat16)
        part = part + jnp.dot(cut_far[k], scaled, preferred_element_type=jnp.float32)
    here = rank % near
    part = part.reshape(near, pad_rows, width)[:, :rows]
    left_over, bit = near, 1
    while left_over > 1:
        low = (here // bit) % 2
        part = part.reshape(left_over // 2, 2, rows, width)
        keep = lax.dynamic_index_in_dim(part, low, 1, keepdims=False)
        give = lax.dynamic_index_in_dim(part, 1 - low, 1, keepdims=False)
        pairs = [(i, i ^ bit) for i in range(n_dp)]
        part = keep + lax.ppermute(give, "dp", pairs)
        left_over, bit = left_over // 2, bit * 2
    return part.reshape(rows, 1, width)


def solution(mesh):
    placed = (
        P(("dp", "expert"), None),
        P(("dp", "expert"), None),
        P(("dp", "expert"), None),
        P("dp", "expert"),
        P("dp", None),
        P("dp", "expert", None, None, None),
    )
    return jax.shard_map(
        shards, mesh=mesh, in_specs=placed, out_specs=P("dp", "expert", None), check_vma=False
    )
```

time: 153 us -> 45.3 us (0.30)
  waiting for transfers between devices: 102 us -> 14.7 us
  starting transfers between devices: 4.24 us -> 23.4 us
  blocking collectives: 14.8 us -> 0 us
  between operations: 14.1 us -> 0.37 us
  local copies, waits for them, and re-layouts: 8.53 us -> 2.37 us
  matrix products: 4.4 us -> 2.06 us
  other arithmetic: 4.2 us -> 2.24 us
    unnamed x2 -> x0, waiting for transfers between devices: 102 us -> none
    ppermute x0 -> x17, starting transfers between devices: none -> 23.4 us  [the longest x12 19.2 us: over_far(): return lax.ppermute(array, 'dp', pairs)]
    ppermute x0 -> x17, waiting for transfers between devices: none -> 14.7 us  [the longest x2 6.72 us: shards(): part = keep + lax.ppermute(give, 'dp', pairs)]
    all_gather x2 -> x0, blocking collectives: 9.81 us -> none  [the longest x1 5.37 us: shards(): lax.all_gather(routes, 'expert', axis=0, tiled=True)]
    psum x1 -> x0, blocking collectives: 4.94 us -> none  [shards(): total_squares = lax.psum(squares, 'expert')]
    transpose x2 -> x0, local copies, waits for them, and re-layouts: 4.59 us -> none  [the longest x1 4.58 us: shards(): jnp.einsum('jif,jid->fjd', acts_slots, scaled, preferred_element_type=jnp...]
    all_to_all x1 -> x0, starting transfers between devices: 4.23 us -> none  [shards(): lax.all_to_all(outgoing, 'expert', split_axis=0, concat_axis=0, tiled=True)]
    dot_general x6 -> x8, matrix products: 4.4 us -> 2.06 us  [the longest x4 1.25 us: shards(): jnp.dot(cut_far[k], scaled, preferred_element_type=jnp.float32)]
  transfers between devices with their start and end apart: 2 -> 17, of which waited for: 1 -> 7; matrix products, arithmetic and copies ran while one was open for 2% -> 7% of each run, Pallas kernels for 0% -> 0%
where the time goes in v1:
time: 45.3 us; the launch traced here: 45.2 us
  starting transfers between devices  23.4 us (52%)
  waiting for transfers between devices  14.7 us (32%)
  local copies, waits for them, and re-layouts  2.37 us (5%)
  other arithmetic  2.24 us (5%)
  matrix products  2.06 us (5%)
    ppermute x12, starting transfers between devices, over_far(): return lax.ppermute(array, 'dp', pairs)  19.2 us
    ppermute x2, waiting for transfers between devices, shards(): part = keep + lax.ppermute(give, 'dp', pairs)  6.72 us
    ppermute x12, waiting for transfers between devices, over_far(): return lax.ppermute(array, 'dp', pairs)  2.94 us
    ppermute x1, waiting for transfers between devices, shards(): lax.ppermute(squares, 'expert', [(s, (s - k) % sources) for s in range(so...  2.81 us
    ppermute x1, waiting for transfers between devices, shards(): rest_rows.append(lax.ppermute(send, 'expert', pairs))  2.21 us
    ppermute x2, starting transfers between devices, shards(): part = keep + lax.ppermute(give, 'dp', pairs)  1.63 us
    ppermute x1, starting transfers between devices, shards(): codes.append(lax.ppermute(send_code, 'expert', pairs))  1.59 us
    unnamed x14, local copies, waits for them, and re-layouts  1.41 us
  transfers between devices with their start and end apart: 17, of which 7 were waited for; matrix products, arithmetic and copies ran while one was open for 7% of the time, Pallas kernels for 0%

profile of v1, /device:TPU:0, one launch (start us, length us, event | category | flops | bytes accessed | tf_op | source)
XLA Modules:
  0.0 45.2 jit_solution(2028074075197621101)
XLA Ops:
  0.0 0.0 copy-start
  0.0 0.0 copy-start.2
  0.0 0.7 %copy-done.4 = s32[1,256]{1,0:T(1,128)S(1)} copy-done((s32[1,256]{1,0:T(1,128)S(1)}, s32[1,256]{1,0:T(1,128)}, u32[]{:S(2)}) %copy-start.4) | copy-done | bytes 1048
  0.7 0.0 copy-done.5
  0.7 0.1 select_reduce_fusion.2
  0.8 0.0 copy-done.3
  0.8 0.0 copy-done.2
  0.9 0.1 fusion.4
  1.0 0.2 fusion.24
  1.2 0.0 copy-done
  1.2 0.3 fusion.1
  1.5 0.0 copy-start.1
  1.5 5.1 %collective-permute-start.13 = (bf16[48,1024]{1,0:T(8,128)(2,1)S(1)}, bf16[48,1024]{1,0:T(8,128)(2,1)S(1)}, u32[]{:S(2)}, u32[]{:S(2)}) collective-permute-start(bf16[48,1024]{1,0:T(8,128)(2,1)S(1)} %get-tuple-element.14), channel_id=1, source_target_pairs={{0,24},{2,26},{4,28},{6,30},{8,0},{10,2},{12,4},{14,6},{16,8},{18,... | collective-permute-start | bytes 294920 | tf_op jit(solution)/shard_map/ppermute | solution.py:67
  6.6 0.0 collective-permute-start.5
  6.6 1.6 %collective-permute-start = (f32[48]{0:T(128)S(1)}, f32[48]{0:T(128)S(1)}, u32[]{:S(2)}, u32[]{:S(2)}) collective-permute-start(f32[48]{0:T(128)S(1)} %get-tuple-element.19), channel_id=1, source_target_pairs={{0,1},{1,0},{2,3},{3,2},{4,5},{5,4},{6,7},{7,6},{8,9},{9,8},{10,11... | collective-permute-start | bytes 584 | tf_op jit(solution)/shard_map/ppermute | solution.py:55
  8.2 0.5 %collective-permute-start.1 = (bf16[48,1024]{1,0:T(8,128)(2,1)S(1)}, bf16[48,1024]{1,0:T(8,128)(2,1)S(1)}, u32[]{:S(2)}, u32[]{:S(2)}) collective-permute-start(bf16[48,1024]{1,0:T(8,128)(2,1)S(1)} %get-tuple-element.15), channel_id=1, source_target_pairs={{0,1},{1,0},{2,3},{3,2},{4,5},{5,4},{6,7},{7,6},{8,9},{9,8},{10,11... | collective-permute-start | bytes 294920 | tf_op jit(solution)/shard_map/ppermute | solution.py:54
  8.7 0.3 concatenate.26
  9.1 0.3 concatenate.27
  9.4 0.3 maximum_bitcast_fusion
  9.7 0.4 copy.22
  10.2 0.1 collective-permute-start.3
  10.3 0.2 fusion.20
  10.5 0.0 collective-permute-done
  10.5 0.1 pad_maximum_fusion.3
  10.6 2.2 %collective-permute-done.1 = bf16[48,1024]{1,0:T(8,128)(2,1)S(1)} collective-permute-done((bf16[48,1024]{1,0:T(8,128)(2,1)S(1)}, bf16[48,1024]{1,0:T(8,128)(2,1)S(1)}, u32[]{:S(2)}, u32[]{:S(2)}) %collective-permute-start.1) | collective-permute-done | bytes 98336 | tf_op jit(solution)/shard_map/ppermute | solution.py:54
  12.8 0.2 select_reduce_fusion
  13.1 0.2 fusion.32
  13.2 0.6 %collective-permute-start.2 = (f32[8]{0:T(128)S(1)}, f32[8]{0:T(128)S(1)}, u32[]{:S(2)}, u32[]{:S(2)}) collective-permute-start(f32[8]{0:T(128)S(1)} %fusion.32), channel_id=1, source_target_pairs={{0,1},{1,0},{2,3},{3,2},{4,5},{5,4},{6,7},{7,6},{8,9},{9,8},{10,11... | collective-permute-start | bytes 104 | tf_op jit(solution)/shard_map/ppermute | solution.py:92
  13.8 0.2 collective-permute-start.6
  14.0 2.8 %collective-permute-done.2 = f32[8]{0:T(128)S(1)} collective-permute-done((f32[8]{0:T(128)S(1)}, f32[8]{0:T(128)S(1)}, u32[]{:S(2)}, u32[]{:S(2)}) %collective-permute-start.2) | collective-permute-done | bytes 64 | tf_op jit(solution)/shard_map/ppermute | solution.py:92
  16.8 0.1 fusion.33
  16.9 0.6 %collective-permute-start.4 = (f32[96]{0:T(128)S(1)}, f32[96]{0:T(128)S(1)}, u32[]{:S(2)}, u32[]{:S(2)}) collective-permute-start(f32[96]{0:T(128)S(1)} %broadcast_multiply_fusion.1), channel_id=1, source_target_pairs={{0,8},{2,10},{4,12},{6,14},{8,16},{10,18},{12,20},{14,22},{16,24},... | collective-permute-start | bytes 1160 | tf_op jit(solution)/shard_map/ppermute | solution.py:67
  17.6 0.3 fusion.5
  17.9 0.0 collective-permute-done.3
  17.9 3.8 %collective-permute-start.9 = (bf16[48,1024]{1,0:T(8,128)(2,1)S(1)}, bf16[48,1024]{1,0:T(8,128)(2,1)S(1)}, u32[]{:S(2)}, u32[]{:S(2)}) collective-permute-start(bf16[48,1024]{1,0:T(8,128)(2,1)S(1)} %get-tuple-element.14), channel_id=1, source_target_pairs={{0,16},{2,18},{4,20},{6,22},{8,24},{10,26},{12,28},{14,30},{16,0},... | collective-permute-start | bytes 294920 | tf_op jit(solution)/shard_map/ppermute | solution.py:67
  21.7 0.0 collective-permute-done.5
  21.7 0.6 %collective-permute-start.11 = (bf16[192,96]{1,0:T(8,128)(2,1)S(1)}, bf16[192,96]{1,0:T(8,128)(2,1)S(1)}, u32[]{:S(2)}, u32[]{:S(2)}) collective-permute-start(bf16[192,96]{1,0:T(8,128)(2,1)S(1)} %get-tuple-element.12), channel_id=1, source_target_pairs={{0,24},{2,26},{4,28},{6,30},{8,0},{10,2},{12,4},{14,6},{16,8},{18,... | collective-permute-start | bytes 110600 | tf_op jit(solution)/shard_map/ppermute | solution.py:67
  22.3 0.1 collective-permute-done.4
  22.4 1.9 %collective-permute-start.14 = (bf16[48,1024]{1,0:T(8,128)(2,1)S(1)}, bf16[48,1024]{1,0:T(8,128)(2,1)S(1)}, u32[]{:S(2)}, u32[]{:S(2)}) collective-permute-start(bf16[48,1024]{1,0:T(8,128)(2,1)S(1)} %collective-permute-done.1), channel_id=1, source_target_pairs={{0,24},{2,26},{4,28},{6,30},{8,0},{10,2},{12,4},{14,6},{16,8},{18,... | collective-permute-start | bytes 294920 | tf_op jit(solution)/shard_map/ppermute | solution.py:67
  24.3 0.0 collective-permute-done.6
  24.3 2.2 %collective-permute-start.12 = (f32[96]{0:T(128)S(1)}, f32[96]{0:T(128)S(1)}, u32[]{:S(2)}, u32[]{:S(2)}) collective-permute-start(f32[96]{0:T(128)S(1)} %broadcast_multiply_fusion.1), channel_id=1, source_target_pairs={{0,24},{2,26},{4,28},{6,30},{8,0},{10,2},{12,4},{14,6},{16,8},{18,... | collective-permute-start | bytes 1160 | tf_op jit(solution)/shard_map/ppermute | solution.py:67
  26.6 0.3 convolution_add_fusion.1
  26.9 0.0 collective-permute-done.11
  26.9 1.6 %collective-permute-start.7 = (bf16[192,96]{1,0:T(8,128)(2,1)S(1)}, bf16[192,96]{1,0:T(8,128)(2,1)S(1)}, u32[]{:S(2)}, u32[]{:S(2)}) collective-permute-start(bf16[192,96]{1,0:T(8,128)(2,1)S(1)} %get-tuple-element.11), channel_id=1, source_target_pairs={{0,16},{2,18},{4,20},{6,22},{8,24},{10,26},{12,28},{14,30},{16,0},... | collective-permute-start | bytes 110600 | tf_op jit(solution)/shard_map/ppermute | solution.py:67
  28.5 0.0 collective-permute-done.13
  28.5 1.4 %collective-permute-start.10 = (bf16[48,1024]{1,0:T(8,128)(2,1)S(1)}, bf16[48,1024]{1,0:T(8,128)(2,1)S(1)}, u32[]{:S(2)}, u32[]{:S(2)}) collective-permute-start(bf16[48,1024]{1,0:T(8,128)(2,1)S(1)} %collective-permute-done.1), channel_id=1, source_target_pairs={{0,16},{2,18},{4,20},{6,22},{8,24},{10,26},{12,28},{14,30},{16,0},... | collective-permute-start | bytes 294920 | tf_op jit(solution)/shard_map/ppermute | solution.py:67
  29.9 0.0 collective-permute-done.12
  29.9 1.5 %collective-permute-start.8 = (f32[96]{0:T(128)S(1)}, f32[96]{0:T(128)S(1)}, u32[]{:S(2)}, u32[]{:S(2)}) collective-permute-start(f32[96]{0:T(128)S(1)} %broadcast_multiply_fusion.1), channel_id=1, source_target_pairs={{0,16},{2,18},{4,20},{6,22},{8,24},{10,26},{12,28},{14,30},{16,0},... | collective-permute-start | bytes 1160 | tf_op jit(solution)/shard_map/ppermute | solution.py:67
  31.4 0.0 collective-permute-done.14
  31.4 0.3 fusion.6
  31.8 0.2 collective-permute-done.7
  32.0 0.0 collective-permute-done.9
  32.0 2.7 %collective-permute-done.8 = f32[96]{0:T(128)S(1)} collective-permute-done((f32[96]{0:T(128)S(1)}, f32[96]{0:T(128)S(1)}, u32[]{:S(2)}, u32[]{:S(2)}) %collective-permute-start.8) | collective-permute-done | bytes 416 | tf_op jit(solution)/shard_map/ppermute | solution.py:67
  34.6 0.0 collective-permute-done.10
  34.6 0.3 fusion
  34.9 0.1 constant_dynamic-slice_fusion.2
  35.0 0.3 copy.27
  35.3 0.1 collective-permute-start.15
  35.4 1.6 %collective-permute-done.15 = f32[2,44,1024]{2,0,1:T(2,128)S(1)} collective-permute-done((f32[2,44,1024]{2,0,1:T(2,128)S(1)}, f32[2,44,1024]{2,0,1:T(2,128)S(1)}, u32[]{:S(2)}, u32[]{:S(2)}) %collective-permute-start.15) | collective-permute-done | bytes 360480 | tf_op jit(solution)/shard_map/ppermute | solution.py:113
  37.1 0.4 fusion.3
  37.4 0.2 constant_dynamic-slice_fusion
  37.6 1.6 %collective-permute-start.16 = (f32[1,44,1024]{2,0,1:T(1,128)S(1)}, f32[1,44,1024]{2,0,1:T(1,128)S(1)}, u32[]{:S(2)}, u32[]{:S(2)}) collective-permute-start(f32[1,44,1024]{2,0,1:T(1,128)S(1)} %constant_dynamic-slice_fusion), channel_id=1, source_target_pairs={{0,4},{2,6},{4,0},{6,2},{8,12},{10,14},{12,8},{14,10},{16,20},{18,... | collective-permute-start | bytes 540680 | tf_op jit(solution)/shard_map/ppermute | solution.py:113
  39.2 5.1 %collective-permute-done.16 = f32[1,44,1024]{2,0,1:T(1,128)S(1)} collective-permute-done((f32[1,44,1024]{2,0,1:T(1,128)S(1)}, f32[1,44,1024]{2,0,1:T(1,128)S(1)}, u32[]{:S(2)}, u32[]{:S(2)}) %collective-permute-start.16) | collective-permute-done | bytes 180256 | tf_op jit(solution)/shard_map/ppermute | solution.py:113
  44.3 0.9 %add_bitcast_fusion = f32[44,1,1024]{2,1,0:T(1,128)} fusion(f32[1,44,1024]{2,0,1:T(1,128)S(1)} %collective-permute-done.16, f32[2,44,1024]{2,0,1:T(2,128)S(1)} %fusion.3, s32[]{:T(128)S(6)} %select_n.118), kind=kLoop, calls=%fused_computation.33 | loop fusion | flops 45056 | bytes 540676 | tf_op jit(solution)/shard_map/reshape | solution.py:115
  (16 shorter events, 0.2 us)
Async XLA Ops:
  0.0 1.2 %copy-start = (bf16[256,1024]{1,0:T(8,128)(2,1)S(1)}, bf16[256,1024]{1,0:T(8,128)(2,1)}, u32[]{:S(2)}) copy-start(bf16[256,1024]{1,0:T(8,128)(2,1)} %param.6) | copy-start | bytes 1572868
  0.0 0.7 %copy-start.4 = (s32[1,256]{1,0:T(1,128)S(1)}, s32[1,256]{1,0:T(1,128)}, u32[]{:S(2)}) copy-start(s32[1,256]{1,0:T(1,128)} %param.9) | copy-start | bytes 3076
  0.0 0.7 %copy-start.5 = (f32[1,8]{1,0:T(1,128)S(1)}, f32[1,8]{1,0:T(1,128)}, u32[]{:S(2)}) copy-start(f32[1,8]{1,0:T(1,128)} %param.10) | copy-start | bytes 100
  0.0 0.8 %copy-start.3 = (f32[256,6]{0,1:T(8,128)S(1)}, f32[256,6]{0,1:T(8,128)}, u32[]{:S(2)}) copy-start(f32[256,6]{0,1:T(8,128)} %param.8) | copy-start | bytes 18436
  0.0 0.8 %copy-start.2 = (s32[256,6]{0,1:T(8,128)S(1)}, s32[256,6]{0,1:T(8,128)}, u32[]{:S(2)}) copy-start(s32[256,6]{0,1:T(8,128)} %param.7) | copy-start | bytes 18436
  1.5 7.3 %copy-start.1 = (bf16[1,1,2,48,704]{4,3,2,1,0:T(8,128)(2,1)S(1)}, bf16[1,1,2,48,704]{4,3,2,1,0:T(8,128)(2,1)}, u32[]{:S(2)}) copy-start(bf16[1,1,2,48,704]{4,3,2,1,0:T(8,128)(2,1)} %param.11) | copy-start | bytes 405508
  1.5 27.0 %collective-permute-start.13 = (bf16[48,1024]{1,0:T(8,128)(2,1)S(1)}, bf16[48,1024]{1,0:T(8,128)(2,1)S(1)}, u32[]{:S(2)}, u32[]{:S(2)}) collective-permute-start(bf16[48,1024]{1,0:T(8,128)(2,1)S(1)} %get-tuple-element.14), channel_id=1, source_target_pairs={{0,24},{2,26},{4,28},{6,30},{8,0},{10,2},{12,4},{14,6},{16,8},{18,... | collective-permute-start | bytes 294920 | tf_op jit(solution)/shard_map/ppermute | solution.py:67
  6.6 15.1 %collective-permute-start.5 = (bf16[48,1024]{1,0:T(8,128)(2,1)S(1)}, bf16[48,1024]{1,0:T(8,128)(2,1)S(1)}, u32[]{:S(2)}, u32[]{:S(2)}) collective-permute-start(bf16[48,1024]{1,0:T(8,128)(2,1)S(1)} %get-tuple-element.14), channel_id=1, source_target_pairs={{0,8},{2,10},{4,12},{6,14},{8,16},{10,18},{12,20},{14,22},{16,24},... | collective-permute-start | bytes 294920 | tf_op jit(solution)/shard_map/ppermute | solution.py:67
  6.6 3.9 %collective-permute-start = (f32[48]{0:T(128)S(1)}, f32[48]{0:T(128)S(1)}, u32[]{:S(2)}, u32[]{:S(2)}) collective-permute-start(f32[48]{0:T(128)S(1)} %get-tuple-element.19), channel_id=1, source_target_pairs={{0,1},{1,0},{2,3},{3,2},{4,5},{5,4},{6,7},{7,6},{8,9},{9,8},{10,11... | collective-permute-start | bytes 584 | tf_op jit(solution)/shard_map/ppermute | solution.py:55
  8.2 4.6 %collective-permute-start.1 = (bf16[48,1024]{1,0:T(8,128)(2,1)S(1)}, bf16[48,1024]{1,0:T(8,128)(2,1)S(1)}, u32[]{:S(2)}, u32[]{:S(2)}) collective-permute-start(bf16[48,1024]{1,0:T(8,128)(2,1)S(1)} %get-tuple-element.15), channel_id=1, source_target_pairs={{0,1},{1,0},{2,3},{3,2},{4,5},{5,4},{6,7},{7,6},{8,9},{9,8},{10,11... | collective-permute-start | bytes 294920 | tf_op jit(solution)/shard_map/ppermute | solution.py:54
  10.2 7.7 %collective-permute-start.3 = (bf16[192,96]{1,0:T(8,128)(2,1)S(1)}, bf16[192,96]{1,0:T(8,128)(2,1)S(1)}, u32[]{:S(2)}, u32[]{:S(2)}) collective-permute-start(bf16[192,96]{1,0:T(8,128)(2,1)S(1)} %get-tuple-element.13), channel_id=1, source_target_pairs={{0,8},{2,10},{4,12},{6,14},{8,16},{10,18},{12,20},{14,22},{16,24},... | collective-permute-start | bytes 110600 | tf_op jit(solution)/shard_map/ppermute | solution.py:67
  13.2 3.6 %collective-permute-start.2 = (f32[8]{0:T(128)S(1)}, f32[8]{0:T(128)S(1)}, u32[]{:S(2)}, u32[]{:S(2)}) collective-permute-start(f32[8]{0:T(128)S(1)} %fusion.32), channel_id=1, source_target_pairs={{0,1},{1,0},{2,3},{3,2},{4,5},{5,4},{6,7},{7,6},{8,9},{9,8},{10,11... | collective-permute-start | bytes 104 | tf_op jit(solution)/shard_map/ppermute | solution.py:92
  13.8 10.5 %collective-permute-start.6 = (bf16[48,1024]{1,0:T(8,128)(2,1)S(1)}, bf16[48,1024]{1,0:T(8,128)(2,1)S(1)}, u32[]{:S(2)}, u32[]{:S(2)}) collective-permute-start(bf16[48,1024]{1,0:T(8,128)(2,1)S(1)} %collective-permute-done.1), channel_id=1, source_target_pairs={{0,8},{2,10},{4,12},{6,14},{8,16},{10,18},{12,20},{14,22},{16,24},... | collective-permute-start | bytes 294920 | tf_op jit(solution)/shard_map/ppermute | solution.py:67
  16.9 5.5 %collective-permute-start.4 = (f32[96]{0:T(128)S(1)}, f32[96]{0:T(128)S(1)}, u32[]{:S(2)}, u32[]{:S(2)}) collective-permute-start(f32[96]{0:T(128)S(1)} %broadcast_multiply_fusion.1), channel_id=1, source_target_pairs={{0,8},{2,10},{4,12},{6,14},{8,16},{10,18},{12,20},{14,22},{16,24},... | collective-permute-start | bytes 1160 | tf_op jit(solution)/shard_map/ppermute | solution.py:67
  17.9 14.1 %collective-permute-start.9 = (bf16[48,1024]{1,0:T(8,128)(2,1)S(1)}, bf16[48,1024]{1,0:T(8,128)(2,1)S(1)}, u32[]{:S(2)}, u32[]{:S(2)}) collective-permute-start(bf16[48,1024]{1,0:T(8,128)(2,1)S(1)} %get-tuple-element.14), channel_id=1, source_target_pairs={{0,16},{2,18},{4,20},{6,22},{8,24},{10,26},{12,28},{14,30},{16,0},... | collective-permute-start | bytes 294920 | tf_op jit(solution)/shard_map/ppermute | solution.py:67
  21.7 5.2 %collective-permute-start.11 = (bf16[192,96]{1,0:T(8,128)(2,1)S(1)}, bf16[192,96]{1,0:T(8,128)(2,1)S(1)}, u32[]{:S(2)}, u32[]{:S(2)}) collective-permute-start(bf16[192,96]{1,0:T(8,128)(2,1)S(1)} %get-tuple-element.12), channel_id=1, source_target_pairs={{0,24},{2,26},{4,28},{6,30},{8,0},{10,2},{12,4},{14,6},{16,8},{18,... | collective-permute-start | bytes 110600 | tf_op jit(solution)/shard_map/ppermute | solution.py:67
  22.4 9.0 %collective-permute-start.14 = (bf16[48,1024]{1,0:T(8,128)(2,1)S(1)}, bf16[48,1024]{1,0:T(8,128)(2,1)S(1)}, u32[]{:S(2)}, u32[]{:S(2)}) collective-permute-start(bf16[48,1024]{1,0:T(8,128)(2,1)S(1)} %collective-permute-done.1), channel_id=1, source_target_pairs={{0,24},{2,26},{4,28},{6,30},{8,0},{10,2},{12,4},{14,6},{16,8},{18,... | collective-permute-start | bytes 294920 | tf_op jit(solution)/shard_map/ppermute | solution.py:67
  24.3 5.6 %collective-permute-start.12 = (f32[96]{0:T(128)S(1)}, f32[96]{0:T(128)S(1)}, u32[]{:S(2)}, u32[]{:S(2)}) collective-permute-start(f32[96]{0:T(128)S(1)} %broadcast_multiply_fusion.1), channel_id=1, source_target_pairs={{0,24},{2,26},{4,28},{6,30},{8,0},{10,2},{12,4},{14,6},{16,8},{18,... | collective-permute-start | bytes 1160 | tf_op jit(solution)/shard_map/ppermute | solution.py:67
  26.9 5.1 %collective-permute-start.7 = (bf16[192,96]{1,0:T(8,128)(2,1)S(1)}, bf16[192,96]{1,0:T(8,128)(2,1)S(1)}, u32[]{:S(2)}, u32[]{:S(2)}) collective-permute-start(bf16[192,96]{1,0:T(8,128)(2,1)S(1)} %get-tuple-element.11), channel_id=1, source_target_pairs={{0,16},{2,18},{4,20},{6,22},{8,24},{10,26},{12,28},{14,30},{16,0},... | collective-permute-start | bytes 110600 | tf_op jit(solution)/shard_map/ppermute | solution.py:67
  28.5 6.1 %collective-permute-start.10 = (bf16[48,1024]{1,0:T(8,128)(2,1)S(1)}, bf16[48,1024]{1,0:T(8,128)(2,1)S(1)}, u32[]{:S(2)}, u32[]{:S(2)}) collective-permute-start(bf16[48,1024]{1,0:T(8,128)(2,1)S(1)} %collective-permute-done.1), channel_id=1, source_target_pairs={{0,16},{2,18},{4,20},{6,22},{8,24},{10,26},{12,28},{14,30},{16,0},... | collective-permute-start | bytes 294920 | tf_op jit(solution)/shard_map/ppermute | solution.py:67
  29.9 4.7 %collective-permute-start.8 = (f32[96]{0:T(128)S(1)}, f32[96]{0:T(128)S(1)}, u32[]{:S(2)}, u32[]{:S(2)}) collective-permute-start(f32[96]{0:T(128)S(1)} %broadcast_multiply_fusion.1), channel_id=1, source_target_pairs={{0,16},{2,18},{4,20},{6,22},{8,24},{10,26},{12,28},{14,30},{16,0},... | collective-permute-start | bytes 1160 | tf_op jit(solution)/shard_map/ppermute | solution.py:67
  35.3 1.7 %collective-permute-start.15 = (f32[2,44,1024]{2,0,1:T(2,128)S(1)}, f32[2,44,1024]{2,0,1:T(2,128)S(1)}, u32[]{:S(2)}, u32[]{:S(2)}) collective-permute-start(f32[2,44,1024]{2,0,1:T(2,128)S(1)} %bitcast.51), channel_id=1, source_target_pairs={{0,2},{2,0},{4,6},{6,4},{8,10},{10,8},{12,14},{14,12},{16,18},{18,... | collective-permute-start | bytes 1081352 | tf_op jit(solution)/shard_map/ppermute | solution.py:113
  37.6 6.7 %collective-permute-start.16 = (f32[1,44,1024]{2,0,1:T(1,128)S(1)}, f32[1,44,1024]{2,0,1:T(1,128)S(1)}, u32[]{:S(2)}, u32[]{:S(2)}) collective-permute-start(f32[1,44,1024]{2,0,1:T(1,128)S(1)} %constant_dynamic-slice_fusion), channel_id=1, source_target_pairs={{0,4},{2,6},{4,0},{6,2},{8,12},{10,14},{12,8},{14,10},{16,20},{18,... | collective-permute-start | bytes 540680 | tf_op jit(solution)/shard_map/ppermute | solution.py:113

commit v2 on v0

v2 whole, which is shorter than its diff:
```python
import jax
import jax.numpy as jnp
from jax import lax
from jax.experimental import pallas as pl
from jax.experimental.pallas import tpu as pltpu
from jax.sharding import PartitionSpec as P

EXAMPLES = 8
FAR = 4
LANES = 128
BF16 = jnp.bfloat16
F32 = jnp.float32


def iota(shape, axis):
    return lax.broadcasted_iota(jnp.int32, shape, axis)


def reversed_bits(p, count):
    return int(format(p, "b").zfill(count)[::-1], 2) if count else 0


def build(sources, cap, routes, weights, ids, loss, grad, own, own_code, *gives):
    me = lax.axis_index("expert")
    tokens, width = grad.shape
    token_ids = ids[...]
    token_weight = jnp.zeros((1, tokens), F32)
    for x in range(EXAMPLES):
        token_weight = jnp.where(token_ids == x, loss[0, x], token_weight)
    token_code = (token_ids + 1).astype(F32)
    hits, scales = [], []
    for k in range(sources):
        match = routes[...] == lax.rem(me + (sources - k), sources)
        hits.append(jnp.sum(jnp.where(match, 1.0, 0.0), axis=0, keepdims=True))
        scales.append(
            jnp.sum(jnp.where(match, weights[...], 0.0), axis=0, keepdims=True) * token_weight
        )
    pad = -(-sources // 8) * 8 - sources
    routed = jnp.concatenate(hits + [jnp.zeros((1, tokens), F32)] * pad, axis=0)
    before = (iota((tokens, tokens), 0) < iota((tokens, tokens), 1)).astype(F32).astype(BF16)
    ranking = jnp.dot(routed.astype(BF16), before, preferred_element_type=F32)
    slot = iota((cap, tokens), 0).astype(F32)
    for k in range(sources):
        placed = jnp.where(ranking[k : k + 1] == slot, hits[k], 0.0)
        slot_scale = jnp.sum(placed * scales[k], axis=1, keepdims=True)
        code = jnp.sum(placed * token_code, axis=1, keepdims=True)
        rows = jnp.dot(placed.astype(BF16), grad[...], preferred_element_type=F32)
        rows = (rows * slot_scale).astype(BF16)
        if k == 0:
            own[...] = rows
            own_code[...] = jnp.broadcast_to(code, (cap, LANES))
        else:
            gives[k - 1][:, :width] = rows
            gives[k - 1][:, width:] = jnp.broadcast_to(code, (cap, LANES)).astype(BF16)


def cut(sources, n_dp, pad, hidden, *outs):
    me, rank = lax.axis_index("expert"), lax.axis_index("dp")
    near = n_dp // FAR
    bits = near.bit_length() - 1
    ff = hidden.shape[2]
    rows = ff // n_dp
    mine, here = rank // near, lax.rem(rank, near)
    column = iota((1, near * pad), 1)
    wanted = jnp.full((1, near * pad), -ff, jnp.int32)
    for p in range(near):
        inside = (column >= p * pad) & (column < p * pad + rows)
        wanted = jnp.where(
            inside, (here ^ reversed_bits(p, bits)) * rows + column - p * pad, wanted
        )
    unit = iota((ff, near * pad), 0)
    acts = [hidden[lax.rem(me + j, sources)] for j in range(sources)]
    acts = jnp.concatenate(acts, axis=0)
    cap = hidden.shape[1]
    for k in range(FAR):
        pick = jnp.where(unit == wanted + (mine ^ k) * (near * rows), 1.0, 0.0).astype(BF16)
        units = jnp.dot(acts, pick, preferred_element_type=F32).astype(BF16)
        for j in range(sources):
            outs[k][:, j * near * pad : (j + 1) * near * pad] = units[j * cap : (j + 1) * cap]


def norms(sources, hidden, own, own_code, *refs):
    takes, squares = refs[: sources - 1], refs[sources - 1]
    me = lax.axis_index("expert")
    width = own.shape[1]
    acts = jnp.concatenate([hidden[lax.rem(me + j, sources)] for j in range(sources)], axis=0)
    cot = jnp.concatenate([own[...]] + [t[:, :width] for t in takes], axis=0)
    member = membership(own_code, takes, width)
    last = (((1,), (1,)), ((), ()))
    left = lax.dot_general(acts, acts, last, preferred_element_type=F32)
    right = lax.dot_general(cot, cot, last, preferred_element_type=F32)
    one_hot = member.astype(BF16)
    alike = lax.dot_general(one_hot, one_hot, last, preferred_element_type=F32)
    per_slot = jnp.sum(left * right * alike, axis=1, keepdims=True)
    squares[...] = jnp.sum(per_slot * member, axis=0, keepdims=True)


def membership(own_code, takes, width):
    code = jnp.concatenate(
        [own_code[...]] + [t[:, width:].astype(F32) for t in takes], axis=0
    )
    lane = iota(code.shape, 1).astype(F32)
    return jnp.where((code == lane) & (code > 0.0), 1.0, 0.0)


def scale(sources, ff, own_code, *refs):
    takes = refs[: sources - 1]
    squares = refs[sources - 1 : 2 * sources - 1]
    rest = refs[2 * sources - 1]
    cap = own_code.shape[0]
    width = takes[0].shape[1] - LANES
    total = squares[0][...]
    for s in squares[1:]:
        total = total + s[...]
    clip = 1.0 / jnp.maximum(jnp.sqrt(total / (ff * width)), 1.0)
    member = membership(own_code, takes, width)
    weight = jnp.sum(member * clip, axis=1, keepdims=True) / EXAMPLES
    for k in range(1, sources):
        part = slice((k - 1) * cap, k * cap)
        slot_weight = weight[k * cap : (k + 1) * cap]
        rest[part, :width] = (slot_weight * takes[k - 1][:, :width].astype(F32)).astype(BF16)
        if k > 1:
            rest[part, width:] = jnp.zeros((cap, LANES), BF16)
    weight = jnp.broadcast_to(weight[:cap], (cap, LANES))
    high = weight.astype(BF16).astype(F32)
    middle = (weight - high).astype(BF16).astype(F32)
    low = weight - high - middle
    lane = iota((cap, LANES), 1)
    three = jnp.where(lane == 0, high, jnp.where(lane == 1, middle, low))
    rest[:cap, width:] = three.astype(BF16)


def product(sources, rows, pad, *refs):
    owns, rests, cuts = refs[:FAR], refs[FAR : 2 * FAR], refs[2 * FAR : 3 * FAR]
    keep, give = refs[3 * FAR : 3 * FAR + 2]
    cots, units = refs[3 * FAR + 2 :]
    cap, width = owns[0].shape
    slots = sources * cap
    for k in range(FAR):
        three = rests[k][:cap, width:].astype(F32)
        weight = three[:, 0:1] + three[:, 1:2] + three[:, 2:3]
        cots[k * slots : k * slots + cap] = (weight * owns[k][...].astype(F32)).astype(BF16)
        cots[k * slots + cap : (k + 1) * slots] = rests[k][:, :width]
        across = units.shape[1]
        for j in range(sources):
            units[k * slots + j * cap : k * slots + (j + 1) * cap] = cuts[k][
                :, j * across : (j + 1) * across
            ]
    half = keep.shape[0]
    pieces = width // LANES
    part = lax.dot_general(
        units[...], cots[...], (((0,), (0,)), ((), ())), preferred_element_type=F32
    )
    for p in range(2 * half):
        out = keep if p < half else give
        for j in range(pieces):
            out[p % half, pl.ds(j, rows, stride=pieces), :] = part[
                p * pad : p * pad + rows, j * LANES : (j + 1) * LANES
            ]


def call(body, outs, args, scalars=(), scratch=(), flops=0):
    vmem = pl.BlockSpec(memory_space=pltpu.VMEM)
    smem = pl.BlockSpec(memory_space=pltpu.SMEM)
    moved = sum(a.size * a.dtype.itemsize for a in args) + sum(
        o.size * o.dtype.itemsize for o in outs
    )
    return pl.pallas_call(
        body,
        out_shape=tuple(outs),
        in_specs=[smem if i in scalars else vmem for i in range(len(args))],
        out_specs=tuple([vmem] * len(outs)),
        scratch_shapes=list(scratch),
        compiler_params=pltpu.CompilerParams(vmem_limit_bytes=32 * 1024 * 1024),
        cost_estimate=pl.CostEstimate(flops=flops, bytes_accessed=moved, transcendentals=0),
    )(*args)


def shards(grad_out, routes, route_weight, example_ids, example_weight, hidden):
    sources = lax.axis_size("expert")
    n_dp = lax.axis_size("dp")
    near = n_dp // FAR
    tokens, width = grad_out.shape
    cap, ff = hidden.shape[3], hidden.shape[4]
    rows = ff // n_dp
    pad = -(-rows // 16) * 16
    while near * pad * sources % LANES:
        pad += 16
    slots = sources * cap
    acts = hidden.reshape(sources, cap, ff)
    shape = jax.ShapeDtypeStruct

    def over_experts(array, k):
        return lax.ppermute(
            array, "expert", [(s, (s - k) % sources) for s in range(sources)]
        )

    def over_far(array, k):
        return lax.ppermute(array, "dp", [(i, i ^ (k * near)) for i in range(n_dp)])

    own, own_code, *gives = call(
        lambda *refs: build(sources, cap, *refs),
        [shape((cap, width), BF16), shape((cap, LANES), F32)]
        + [shape((cap, width + LANES), BF16)] * (sources - 1),
        (routes.T, route_weight.T, example_ids, example_weight, grad_out),
        scalars=(3,),
        flops=2 * slots * tokens * width,
    )
    takes = [over_experts(g, k + 1) for k, g in enumerate(gives)]
    owns = [own, over_far(own, 1), over_far(own, 2)]

    cuts = call(
        lambda *refs: cut(sources, n_dp, pad, *refs),
        [shape((cap, sources * near * pad), BF16)] * FAR,
        (acts,),
        flops=2 * slots * ff * near * pad * FAR,
    )
    cuts = [cuts[0]] + [over_far(cuts[k], k) for k in range(1, FAR)]
    owns.append(over_far(owns[2], 1))

    (squares,) = call(
        lambda *refs: norms(sources, *refs),
        [shape((1, LANES), F32)],
        (acts, own, own_code, *takes),
        flops=2 * slots * slots * (ff + width),
    )
    all_squares = [squares] + [over_experts(squares, k) for k in range(1, sources)]
    (rest,) = call(
        lambda *refs: scale(sources, ff, *refs),
        [shape((slots - cap, width + LANES), BF16)],
        (own_code, *takes, *all_squares),
        flops=slots * width,
    )
    rests = [rest, over_far(rest, 1), None, over_far(rest, 3)]
    rests[2] = over_far(rests[3], 1)

    keep, give = call(
        lambda *refs: product(sources, rows, pad, *refs),
        [shape((near // 2, rows * (width // LANES), LANES), F32)] * 2,
        (*owns, *rests, *cuts),
        scratch=(
            pltpu.VMEM((FAR * slots, width), BF16),
            pltpu.VMEM((FAR * slots, near * pad), BF16),
        ),
        flops=2 * FAR * slots * near * pad * width,
    )
    bit = 1
    while True:
        part = keep + lax.ppermute(give, "dp", [(i, i ^ bit) for i in range(n_dp)])
        half = part.shape[0] // 2
        if half == 0:
            break
        keep, give, bit = part[:half], part[half:], bit * 2
    return part.reshape(rows, 1, width)


def solution(mesh):
    placed = (
        P(("dp", "expert"), None),
        P(("dp", "expert"), None),
        P(("dp", "expert"), None),
        P("dp", "expert"),
        P("dp", None),
        P("dp", "expert", None, None, None),
    )
    return jax.shard_map(
        shards, mesh=mesh, in_specs=placed, out_specs=P("dp", "expert", None), check_vma=False
    )
```

time: 153 us -> 47.4 us (0.31)
  waiting for transfers between devices: 102 us -> 19.7 us
  starting transfers between devices: 4.24 us -> 20.9 us
  blocking collectives: 14.8 us -> 0 us
  between operations: 14.1 us -> 0.07 us
  local copies, waits for them, and re-layouts: 8.53 us -> 3.13 us
  matrix products: 4.4 us -> 0 us
  other arithmetic: 4.2 us -> 0.75 us
  Pallas kernels: 0 us -> 2.54 us
    unnamed x2 -> x0, waiting for transfers between devices: 102 us -> none
    ppermute x0 -> x13, starting transfers between devices: none -> 20.9 us  [the longest x9 14.5 us: over_far(): return lax.ppermute(array, 'dp', [(i, i ^ k * near) for i in range(n_dp)])]
    ppermute x0 -> x13, waiting for transfers between devices: none -> 19.7 us  [the longest x9 8.1 us: over_far(): return lax.ppermute(array, 'dp', [(i, i ^ k * near) for i in range(n_dp)])]
    all_gather x2 -> x0, blocking collectives: 9.81 us -> none  [the longest x1 5.37 us: shards(): lax.all_gather(routes, 'expert', axis=0, tiled=True)]
    psum x1 -> x0, blocking collectives: 4.94 us -> none  [shards(): total_squares = lax.psum(squares, 'expert')]
    transpose x2 -> x0, local copies, waits for them, and re-layouts: 4.59 us -> none  [the longest x1 4.58 us: shards(): jnp.einsum('jif,jid->fjd', acts_slots, scaled, preferred_element_type=jnp...]
    dot_general x6 -> x0, matrix products: 4.4 us -> none  [the longest x1 1.53 us: shards(): jnp.einsum('jif,jid->fjd', acts_slots, scaled, preferred_element_type=jnp...]
    all_to_all x1 -> x0, starting transfers between devices: 4.23 us -> none  [shards(): lax.all_to_all(outgoing, 'expert', split_axis=0, concat_axis=0, tiled=True)]
  transfers between devices with their start and end apart: 2 -> 13, of which waited for: 1 -> 8; matrix products, arithmetic and copies ran while one was open for 2% -> 0% of each run, Pallas kernels for 0% -> 1%
where the time goes in v2:
time: 47.4 us; the launch traced here: 47.1 us
  starting transfers between devices  20.9 us (44%)
  waiting for transfers between devices  19.7 us (42%)
  local copies, waits for them, and re-layouts  3.13 us (7%)
  Pallas kernels  2.54 us (5%)
  other arithmetic  0.75 us (2%)
    ppermute x9, starting transfers between devices, over_far(): return lax.ppermute(array, 'dp', [(i, i ^ k * near) for i in range(n_dp)])  14.5 us
    ppermute x9, waiting for transfers between devices, over_far(): return lax.ppermute(array, 'dp', [(i, i ^ k * near) for i in range(n_dp)])  8.1 us
    ppermute x2, waiting for transfers between devices, shards(): part = keep + lax.ppermute(give, 'dp', [(i, i ^ bit) for i in range(n_dp)])  6.76 us
    ppermute x2, waiting for transfers between devices, over_experts(): lax.ppermute(array, 'expert', [(s, (s - k) % sources) for s in range(sour...  4.85 us
    ppermute x2, starting transfers between devices, over_experts(): lax.ppermute(array, 'expert', [(s, (s - k) % sources) for s in range(sour...  4.82 us
    unnamed x12, local copies, waits for them, and re-layouts  3.12 us
    pallas_call x5, Pallas kernels, call(): pl.pallas_call(body, out_shape=tuple(outs), in_specs=[smem if i in scalar...  2.54 us
    ppermute x2, starting transfers between devices, shards(): part = keep + lax.ppermute(give, 'dp', [(i, i ^ bit) for i in range(n_dp)])  1.64 us
  transfers between devices with their start and end apart: 13, of which 8 were waited for; matrix products, arithmetic and copies ran while one was open for 0% of the time, Pallas kernels for 1%

profile of v2, /device:TPU:0, one launch (start us, length us, event | category | flops | bytes accessed | tf_op | source)
XLA Modules:
  0.0 47.1 jit_solution(1537699356773787610)
XLA Ops:
  0.0 0.0 copy-start.4
  0.0 0.0 copy-start.5
  0.0 0.7 %copy-done.4 = s32[1,256]{1,0:T(1,128)S(1)} copy-done((s32[1,256]{1,0:T(1,128)S(1)}, s32[1,256]{1,0:T(1,128)}, u32[]{:S(2)}) %copy-start.4) | copy-done | bytes 1048
  0.7 0.0 copy-done.5
  0.7 0.0 copy-start
  0.7 1.0 %copy-done = bf16[256,1024]{1,0:T(8,128)(2,1)S(1)} copy-done((bf16[256,1024]{1,0:T(8,128)(2,1)S(1)}, bf16[256,1024]{1,0:T(8,128)(2,1)}, u32[]{:S(2)}) %copy-start) | copy-done | bytes 524312
  1.7 0.0 copy-start.2
  1.7 0.7 %copy-done.2 = s32[256,6]{0,1:T(8,128)S(1)} copy-done((s32[256,6]{0,1:T(8,128)S(1)}, s32[256,6]{0,1:T(8,128)}, u32[]{:S(2)}) %copy-start.2) | copy-done | bytes 6168
  2.4 0.0 copy-start.3
  2.4 0.7 %copy-done.3 = f32[256,6]{0,1:T(8,128)S(1)} copy-done((f32[256,6]{0,1:T(8,128)S(1)}, f32[256,6]{0,1:T(8,128)}, u32[]{:S(2)}) %copy-start.3) | copy-done | bytes 6168
  3.1 0.0 copy-start.1
  3.1 1.0 %shard_map.64 = (bf16[48,1024]{1,0:T(8,128)(2,1)S(1)}, f32[48,128]{1,0:T(8,128)S(1)}, bf16[48,1152]{1,0:T(8,128)(2,1)S(1)}) custom-call(s32[6,256]{1,0:T(8,128)S(1)} %bitcast.6, f32[6,256]{1,0:T(8,128)S(1)} %bitcast.7, s32[1,256]{1,0:T(1,128)S(1)} %copy-done.4, f32[1,8]{1,0:T(1,128)S(1)} %copy-done.5, bf16[256,1024]{1,0:T(8,128)(2,1)S(1)} %copy-done), custom_call_target="tpu_custom_call" | custom-call | flops 50331648 | bytes 771104 | tf_op jit(solution)/shard_map/pallas_call | solution.py:168
  4.1 3.0 %collective-permute-start.3 = (bf16[48,1152]{1,0:T(8,128)(2,1)S(1)}, bf16[48,1152]{1,0:T(8,128)(2,1)S(1)}, u32[]{:S(2)}, u32[]{:S(2)}) collective-permute-start(bf16[48,1152]{1,0:T(8,128)(2,1)S(1)} %get-tuple-element.16), channel_id=1, source_target_pairs={{0,1},{1,0},{2,3},{3,2},{4,5},{5,4},{6,7},{7,6},{8,9},{9,8},{10,11... | collective-permute-start | bytes 331784 | tf_op jit(solution)/shard_map/ppermute | solution.py:194
  7.1 3.1 %collective-permute-done.3.refs_3_.refs_1_ = bf16[48,1152]{1,0:T(8,128)(2,1)S(1)} collective-permute-done((bf16[48,1152]{1,0:T(8,128)(2,1)S(1)}, bf16[48,1152]{1,0:T(8,128)(2,1)S(1)}, u32[]{:S(2)}, u32[]{:S(2)}) %collective-permute-start.3) | collective-permute-done | bytes 110624 | tf_op jit(solution)/shard_map/ppermute | solution.py:194
  10.2 0.0 copy-done.1
  10.2 0.3 shard_map.65.refs_2_
  10.5 1.8 %collective-permute-start.4 = (f32[1,128]{1,0:T(1,128)S(1)}, f32[1,128]{1,0:T(1,128)S(1)}, u32[]{:S(2)}, u32[]{:S(2)}) collective-permute-start(f32[1,128]{1,0:T(1,128)S(1)} %shard_map.65.refs_2_), channel_id=1, source_target_pairs={{0,1},{1,0},{2,3},{3,2},{4,5},{5,4},{6,7},{7,6},{8,9},{9,8},{10,11... | collective-permute-start | bytes 1544 | tf_op jit(solution)/shard_map/ppermute | solution.py:194
  12.3 1.8 %collective-permute-done.4.refs_3_ = f32[1,128]{1,0:T(1,128)S(1)} collective-permute-done((f32[1,128]{1,0:T(1,128)S(1)}, f32[1,128]{1,0:T(1,128)S(1)}, u32[]{:S(2)}, u32[]{:S(2)}) %collective-permute-start.4) | collective-permute-done | bytes 544 | tf_op jit(solution)/shard_map/ppermute | solution.py:194
  14.1 0.1 shard_map.66.refs_4_
  14.3 3.9 %collective-permute-start.6 = (bf16[48,1152]{1,0:T(8,128)(2,1)S(1)}, bf16[48,1152]{1,0:T(8,128)(2,1)S(1)}, u32[]{:S(2)}, u32[]{:S(2)}) collective-permute-start(bf16[48,1152]{1,0:T(8,128)(2,1)S(1)} %shard_map.66.refs_4_), channel_id=1, source_target_pairs={{0,24},{2,26},{4,28},{6,30},{8,16},{10,18},{12,20},{14,22},{16,8},... | collective-permute-start | bytes 331784 | tf_op jit(solution)/shard_map/ppermute | solution.py:199
  18.2 0.0 collective-permute-start.1
  18.2 0.5 shard_map.67
  18.6 0.7 %collective-permute-start.8 = (bf16[48,384]{1,0:T(8,128)(2,1)S(1)}, bf16[48,384]{1,0:T(8,128)(2,1)S(1)}, u32[]{:S(2)}, u32[]{:S(2)}) collective-permute-start(bf16[48,384]{1,0:T(8,128)(2,1)S(1)} %get-tuple-element.18), channel_id=1, source_target_pairs={{0,8},{2,10},{4,12},{6,14},{8,0},{10,2},{12,4},{14,6},{16,24},{18,... | collective-permute-start | bytes 110600 | tf_op jit(solution)/shard_map/ppermute | solution.py:199
  19.3 1.4 %collective-permute-start.5 = (bf16[48,1152]{1,0:T(8,128)(2,1)S(1)}, bf16[48,1152]{1,0:T(8,128)(2,1)S(1)}, u32[]{:S(2)}, u32[]{:S(2)}) collective-permute-start(bf16[48,1152]{1,0:T(8,128)(2,1)S(1)} %shard_map.66.refs_4_), channel_id=1, source_target_pairs={{0,8},{2,10},{4,12},{6,14},{8,0},{10,2},{12,4},{14,6},{16,24},{18,... | collective-permute-start | bytes 331784 | tf_op jit(solution)/shard_map/ppermute | solution.py:199
  20.7 0.9 %collective-permute-done.6.refs_7_ = bf16[48,1152]{1,0:T(8,128)(2,1)S(1)} collective-permute-done((bf16[48,1152]{1,0:T(8,128)(2,1)S(1)}, bf16[48,1152]{1,0:T(8,128)(2,1)S(1)}, u32[]{:S(2)}, u32[]{:S(2)}) %collective-permute-start.6) | collective-permute-done | bytes 110624 | tf_op jit(solution)/shard_map/ppermute | solution.py:199
  21.7 2.8 %collective-permute-start.7 = (bf16[48,1152]{1,0:T(8,128)(2,1)S(1)}, bf16[48,1152]{1,0:T(8,128)(2,1)S(1)}, u32[]{:S(2)}, u32[]{:S(2)}) collective-permute-start(bf16[48,1152]{1,0:T(8,128)(2,1)S(1)} %collective-permute-done.6.refs_7_), channel_id=1, source_target_pairs={{0,8},{2,10},{4,12},{6,14},{8,0},{10,2},{12,4},{14,6},{16,24},{18,... | collective-permute-start | bytes 331784 | tf_op jit(solution)/shard_map/ppermute | solution.py:199
  24.5 0.0 collective-permute-start
  24.5 0.5 %collective-permute-done.1.refs_2_ = bf16[48,1024]{1,0:T(8,128)(2,1)S(1)} collective-permute-done((bf16[48,1024]{1,0:T(8,128)(2,1)S(1)}, bf16[48,1024]{1,0:T(8,128)(2,1)S(1)}, u32[]{:S(2)}, u32[]{:S(2)}) %collective-permute-start.1) | collective-permute-done | bytes 98336 | tf_op jit(solution)/shard_map/ppermute | solution.py:199
  25.0 1.5 %collective-permute-start.2 = (bf16[48,1024]{1,0:T(8,128)(2,1)S(1)}, bf16[48,1024]{1,0:T(8,128)(2,1)S(1)}, u32[]{:S(2)}, u32[]{:S(2)}) collective-permute-start(bf16[48,1024]{1,0:T(8,128)(2,1)S(1)} %collective-permute-done.1.refs_2_), channel_id=1, source_target_pairs={{0,8},{2,10},{4,12},{6,14},{8,0},{10,2},{12,4},{14,6},{16,24},{18,... | collective-permute-start | bytes 294920 | tf_op jit(solution)/shard_map/ppermute | solution.py:199
  26.5 0.0 collective-permute-done.8.refs_9_
  26.5 2.1 %collective-permute-start.9 = (bf16[48,384]{1,0:T(8,128)(2,1)S(1)}, bf16[48,384]{1,0:T(8,128)(2,1)S(1)}, u32[]{:S(2)}, u32[]{:S(2)}) collective-permute-start(bf16[48,384]{1,0:T(8,128)(2,1)S(1)} %get-tuple-element.19), channel_id=1, source_target_pairs={{0,16},{2,18},{4,20},{6,22},{8,24},{10,26},{12,28},{14,30},{16,0},... | collective-permute-start | bytes 110600 | tf_op jit(solution)/shard_map/ppermute | solution.py:199
  28.6 2.9 %collective-permute-done.9.refs_10_ = bf16[48,384]{1,0:T(8,128)(2,1)S(1)} collective-permute-done((bf16[48,384]{1,0:T(8,128)(2,1)S(1)}, bf16[48,384]{1,0:T(8,128)(2,1)S(1)}, u32[]{:S(2)}, u32[]{:S(2)}) %collective-permute-start.9) | collective-permute-done | bytes 36896 | tf_op jit(solution)/shard_map/ppermute | solution.py:199
  31.5 2.1 %collective-permute-start.10 = (bf16[48,384]{1,0:T(8,128)(2,1)S(1)}, bf16[48,384]{1,0:T(8,128)(2,1)S(1)}, u32[]{:S(2)}, u32[]{:S(2)}) collective-permute-start(bf16[48,384]{1,0:T(8,128)(2,1)S(1)} %get-tuple-element.20), channel_id=1, source_target_pairs={{0,24},{2,26},{4,28},{6,30},{8,16},{10,18},{12,20},{14,22},{16,8},... | collective-permute-start | bytes 110600 | tf_op jit(solution)/shard_map/ppermute | solution.py:199
  33.6 3.7 %collective-permute-done.10.refs_11_ = bf16[48,384]{1,0:T(8,128)(2,1)S(1)} collective-permute-done((bf16[48,384]{1,0:T(8,128)(2,1)S(1)}, bf16[48,384]{1,0:T(8,128)(2,1)S(1)}, u32[]{:S(2)}, u32[]{:S(2)}) %collective-permute-start.10) | collective-permute-done | bytes 36896 | tf_op jit(solution)/shard_map/ppermute | solution.py:199
  37.3 0.0 collective-permute-done.refs_1_
  37.3 0.0 collective-permute-done.2.refs_3_
  37.3 0.0 collective-permute-done.5.refs_5_
  37.3 0.0 collective-permute-done.7.refs_6_
  37.3 0.6 %shard_map.68 = (f32[2,352,128]{2,1,0:T(8,128)S(1)}, f32[2,352,128]{2,1,0:T(8,128)S(1)}) custom-call(bf16[48,1024]{1,0:T(8,128)(2,1)S(1)} %get-tuple-element.14.refs_1_.refs_0_, bf16[48,1024]{1,0:T(8,128)(2,1)S(1)} %collective-permute-done.refs_1_, bf16[48,1024]{1,0:T(8,128)(2,1)S(1)} %collective-permute-done.1.refs_2_, ...), custom_call_target="tpu_custom_call" | custom-call | flops 150994944 | bytes 1703936 | tf_op jit(solution)/shard_map/pallas_call | solution.py:168
  37.9 0.1 collective-permute-start.11
  38.0 1.7 %collective-permute-done.11 = f32[2,352,128]{2,1,0:T(8,128)S(1)} collective-permute-done((f32[2,352,128]{2,1,0:T(8,128)S(1)}, f32[2,352,128]{2,1,0:T(8,128)S(1)}, u32[]{:S(2)}, u32[]{:S(2)}) %collective-permute-start.11) | collective-permute-done | bytes 360480 | tf_op jit(solution)/shard_map/ppermute | solution.py:249
  39.7 0.1 add.6
  39.8 1.6 %collective-permute-start.12 = (f32[1,352,128]{2,1,0:T(8,128)S(1)}, f32[1,352,128]{2,1,0:T(8,128)S(1)}, u32[]{:S(2)}, u32[]{:S(2)}) collective-permute-start(f32[1,352,128]{2,1,0:T(8,128)S(1)} %slice.9), channel_id=1, source_target_pairs={{0,4},{2,6},{4,0},{6,2},{8,12},{10,14},{12,8},{14,10},{16,20},{18,... | collective-permute-start | bytes 540680 | tf_op jit(solution)/shard_map/ppermute | solution.py:249
  41.3 5.1 %collective-permute-done.12 = f32[1,352,128]{2,1,0:T(8,128)S(1)} collective-permute-done((f32[1,352,128]{2,1,0:T(8,128)S(1)}, f32[1,352,128]{2,1,0:T(8,128)S(1)}, u32[]{:S(2)}, u32[]{:S(2)}) %collective-permute-start.12) | collective-permute-done | bytes 180256 | tf_op jit(solution)/shard_map/ppermute | solution.py:249
  46.4 0.7 %slice_add_fusion = f32[1,352,128]{2,1,0:T(8,128)} fusion(f32[1,352,128]{2,1,0:T(8,128)S(1)} %collective-permute-done.12, f32[2,352,128]{2,1,0:T(8,128)S(1)} %add.6), kind=kLoop, calls=%fused_computation | loop fusion | flops 45056 | bytes 540672 | tf_op jit(solution)/shard_map/add | solution.py:249
  (1 shorter events, 0.0 us)
Async XLA Ops:
  0.0 0.7 %copy-start.4 = (s32[1,256]{1,0:T(1,128)S(1)}, s32[1,256]{1,0:T(1,128)}, u32[]{:S(2)}) copy-start(s32[1,256]{1,0:T(1,128)} %refs_2_.1) | copy-start | bytes 3076
  0.0 0.7 %copy-start.5 = (f32[1,8]{1,0:T(1,128)S(1)}, f32[1,8]{1,0:T(1,128)}, u32[]{:S(2)}) copy-start(f32[1,8]{1,0:T(1,128)} %refs_3_.1) | copy-start | bytes 100
  0.7 1.0 %copy-start = (bf16[256,1024]{1,0:T(8,128)(2,1)S(1)}, bf16[256,1024]{1,0:T(8,128)(2,1)}, u32[]{:S(2)}) copy-start(bf16[256,1024]{1,0:T(8,128)(2,1)} %refs_4_.1) | copy-start | bytes 1572868
  1.7 0.7 %copy-start.2 = (s32[256,6]{0,1:T(8,128)S(1)}, s32[256,6]{0,1:T(8,128)}, u32[]{:S(2)}) copy-start(s32[256,6]{0,1:T(8,128)} %param.7) | copy-start | bytes 18436
  2.4 0.7 %copy-start.3 = (f32[256,6]{0,1:T(8,128)S(1)}, f32[256,6]{0,1:T(8,128)}, u32[]{:S(2)}) copy-start(f32[256,6]{0,1:T(8,128)} %param.8) | copy-start | bytes 18436
  3.1 7.1 %copy-start.1 = (bf16[1,1,2,48,704]{4,3,2,1,0:T(8,128)(2,1)S(1)}, bf16[1,1,2,48,704]{4,3,2,1,0:T(8,128)(2,1)}, u32[]{:S(2)}) copy-start(bf16[1,1,2,48,704]{4,3,2,1,0:T(8,128)(2,1)} %param.11) | copy-start | bytes 405508
  4.1 6.1 %collective-permute-start.3 = (bf16[48,1152]{1,0:T(8,128)(2,1)S(1)}, bf16[48,1152]{1,0:T(8,128)(2,1)S(1)}, u32[]{:S(2)}, u32[]{:S(2)}) collective-permute-start(bf16[48,1152]{1,0:T(8,128)(2,1)S(1)} %get-tuple-element.16), channel_id=1, source_target_pairs={{0,1},{1,0},{2,3},{3,2},{4,5},{5,4},{6,7},{7,6},{8,9},{9,8},{10,11... | collective-permute-start | bytes 331784 | tf_op jit(solution)/shard_map/ppermute | solution.py:194
  10.5 3.6 %collective-permute-start.4 = (f32[1,128]{1,0:T(1,128)S(1)}, f32[1,128]{1,0:T(1,128)S(1)}, u32[]{:S(2)}, u32[]{:S(2)}) collective-permute-start(f32[1,128]{1,0:T(1,128)S(1)} %shard_map.65.refs_2_), channel_id=1, source_target_pairs={{0,1},{1,0},{2,3},{3,2},{4,5},{5,4},{6,7},{7,6},{8,9},{9,8},{10,11... | collective-permute-start | bytes 1544 | tf_op jit(solution)/shard_map/ppermute | solution.py:194
  14.3 7.4 %collective-permute-start.6 = (bf16[48,1152]{1,0:T(8,128)(2,1)S(1)}, bf16[48,1152]{1,0:T(8,128)(2,1)S(1)}, u32[]{:S(2)}, u32[]{:S(2)}) collective-permute-start(bf16[48,1152]{1,0:T(8,128)(2,1)S(1)} %shard_map.66.refs_4_), channel_id=1, source_target_pairs={{0,24},{2,26},{4,28},{6,30},{8,16},{10,18},{12,20},{14,22},{16,8},... | collective-permute-start | bytes 331784 | tf_op jit(solution)/shard_map/ppermute | solution.py:199
  18.2 6.9 %collective-permute-start.1 = (bf16[48,1024]{1,0:T(8,128)(2,1)S(1)}, bf16[48,1024]{1,0:T(8,128)(2,1)S(1)}, u32[]{:S(2)}, u32[]{:S(2)}) collective-permute-start(bf16[48,1024]{1,0:T(8,128)(2,1)S(1)} %get-tuple-element.14.refs_1_.refs_0_), channel_id=1, source_target_pairs={{0,16},{2,18},{4,20},{6,22},{8,24},{10,26},{12,28},{14,30},{16,0},... | collective-permute-start | bytes 294920 | tf_op jit(solution)/shard_map/ppermute | solution.py:199
  18.6 7.9 %collective-permute-start.8 = (bf16[48,384]{1,0:T(8,128)(2,1)S(1)}, bf16[48,384]{1,0:T(8,128)(2,1)S(1)}, u32[]{:S(2)}, u32[]{:S(2)}) collective-permute-start(bf16[48,384]{1,0:T(8,128)(2,1)S(1)} %get-tuple-element.18), channel_id=1, source_target_pairs={{0,8},{2,10},{4,12},{6,14},{8,0},{10,2},{12,4},{14,6},{16,24},{18,... | collective-permute-start | bytes 110600 | tf_op jit(solution)/shard_map/ppermute | solution.py:199
  19.3 18.0 %collective-permute-start.5 = (bf16[48,1152]{1,0:T(8,128)(2,1)S(1)}, bf16[48,1152]{1,0:T(8,128)(2,1)S(1)}, u32[]{:S(2)}, u32[]{:S(2)}) collective-permute-start(bf16[48,1152]{1,0:T(8,128)(2,1)S(1)} %shard_map.66.refs_4_), channel_id=1, source_target_pairs={{0,8},{2,10},{4,12},{6,14},{8,0},{10,2},{12,4},{14,6},{16,24},{18,... | collective-permute-start | bytes 331784 | tf_op jit(solution)/shard_map/ppermute | solution.py:199
  21.7 15.6 %collective-permute-start.7 = (bf16[48,1152]{1,0:T(8,128)(2,1)S(1)}, bf16[48,1152]{1,0:T(8,128)(2,1)S(1)}, u32[]{:S(2)}, u32[]{:S(2)}) collective-permute-start(bf16[48,1152]{1,0:T(8,128)(2,1)S(1)} %collective-permute-done.6.refs_7_), channel_id=1, source_target_pairs={{0,8},{2,10},{4,12},{6,14},{8,0},{10,2},{12,4},{14,6},{16,24},{18,... | collective-permute-start | bytes 331784 | tf_op jit(solution)/shard_map/ppermute | solution.py:199
  24.5 12.8 %collective-permute-start = (bf16[48,1024]{1,0:T(8,128)(2,1)S(1)}, bf16[48,1024]{1,0:T(8,128)(2,1)S(1)}, u32[]{:S(2)}, u32[]{:S(2)}) collective-permute-start(bf16[48,1024]{1,0:T(8,128)(2,1)S(1)} %get-tuple-element.14.refs_1_.refs_0_), channel_id=1, source_target_pairs={{0,8},{2,10},{4,12},{6,14},{8,0},{10,2},{12,4},{14,6},{16,24},{18,... | collective-permute-start | bytes 294920 | tf_op jit(solution)/shard_map/ppermute | solution.py:199
  25.0 12.3 %collective-permute-start.2 = (bf16[48,1024]{1,0:T(8,128)(2,1)S(1)}, bf16[48,1024]{1,0:T(8,128)(2,1)S(1)}, u32[]{:S(2)}, u32[]{:S(2)}) collective-permute-start(bf16[48,1024]{1,0:T(8,128)(2,1)S(1)} %collective-permute-done.1.refs_2_), channel_id=1, source_target_pairs={{0,8},{2,10},{4,12},{6,14},{8,0},{10,2},{12,4},{14,6},{16,24},{18,... | collective-permute-start | bytes 294920 | tf_op jit(solution)/shard_map/ppermute | solution.py:199
  26.5 5.0 %collective-permute-start.9 = (bf16[48,384]{1,0:T(8,128)(2,1)S(1)}, bf16[48,384]{1,0:T(8,128)(2,1)S(1)}, u32[]{:S(2)}, u32[]{:S(2)}) collective-permute-start(bf16[48,384]{1,0:T(8,128)(2,1)S(1)} %get-tuple-element.19), channel_id=1, source_target_pairs={{0,16},{2,18},{4,20},{6,22},{8,24},{10,26},{12,28},{14,30},{16,0},... | collective-permute-start | bytes 110600 | tf_op jit(solution)/shard_map/ppermute | solution.py:199
  31.5 5.8 %collective-permute-start.10 = (bf16[48,384]{1,0:T(8,128)(2,1)S(1)}, bf16[48,384]{1,0:T(8,128)(2,1)S(1)}, u32[]{:S(2)}, u32[]{:S(2)}) collective-permute-start(bf16[48,384]{1,0:T(8,128)(2,1)S(1)} %get-tuple-element.20), channel_id=1, source_target_pairs={{0,24},{2,26},{4,28},{6,30},{8,16},{10,18},{12,20},{14,22},{16,8},... | collective-permute-start | bytes 110600 | tf_op jit(solution)/shard_map/ppermute | solution.py:199
  37.9 1.7 %collective-permute-start.11 = (f32[2,352,128]{2,1,0:T(8,128)S(1)}, f32[2,352,128]{2,1,0:T(8,128)S(1)}, u32[]{:S(2)}, u32[]{:S(2)}) collective-permute-start(f32[2,352,128]{2,1,0:T(8,128)S(1)} %get-tuple-element.22), channel_id=1, source_target_pairs={{0,2},{2,0},{4,6},{6,4},{8,10},{10,8},{12,14},{14,12},{16,18},{18,... | collective-permute-start | bytes 1081352 | tf_op jit(solution)/shard_map/ppermute | solution.py:249
  39.8 6.7 %collective-permute-start.12 = (f32[1,352,128]{2,1,0:T(8,128)S(1)}, f32[1,352,128]{2,1,0:T(8,128)S(1)}, u32[]{:S(2)}, u32[]{:S(2)}) collective-permute-start(f32[1,352,128]{2,1,0:T(8,128)S(1)} %slice.9), channel_id=1, source_target_pairs={{0,4},{2,6},{4,0},{6,2},{8,12},{10,14},{12,8},{14,10},{16,20},{18,... | collective-permute-start | bytes 540680 | tf_op jit(solution)/shard_map/ppermute | solution.py:249

commit v3 on v2

v3 whole, which is shorter than its diff:
```python
import jax
import jax.numpy as jnp
from jax import lax
from jax.experimental import pallas as pl
from jax.experimental.pallas import tpu as pltpu
from jax.sharding import PartitionSpec as P

EXAMPLES = 8
FAR = 4
LANES = 128
BF16 = jnp.bfloat16
F32 = jnp.float32


def iota(shape, axis):
    return lax.broadcasted_iota(jnp.int32, shape, axis)


def reversed_bits(p, count):
    return int(format(p, "b").zfill(count)[::-1], 2) if count else 0


def build(sources, cap, routes_at, weights_at, ids_at, loss_at, grad_at, own, own_code, *refs):
    gives = refs[: sources - 1]
    routes, weights, ids, loss, grad, sems = refs[sources - 1 :]
    fetches = [
        pltpu.make_async_copy(source, target, sems.at[i])
        for i, (source, target) in enumerate(
            [
                (routes_at, routes),
                (ids_at, ids),
                (loss_at, loss),
                (weights_at, weights),
                (grad_at, grad),
            ]
        )
    ]
    for fetch in fetches:
        fetch.start()
    me = lax.axis_index("expert")
    tokens, width = grad.shape
    before = (iota((tokens, tokens), 0) < iota((tokens, tokens), 1)).astype(F32).astype(BF16)
    slot = iota((cap, tokens), 0).astype(F32)
    fetches[0].wait()
    matches = [routes[...] == lax.rem(me + (sources - k), sources) for k in range(sources)]
    hits = [jnp.sum(jnp.where(m, 1.0, 0.0), axis=0, keepdims=True) for m in matches]
    pad = -(-sources // 8) * 8 - sources
    routed = jnp.concatenate(hits + [jnp.zeros((1, tokens), F32)] * pad, axis=0)
    ranking = jnp.dot(routed.astype(BF16), before, preferred_element_type=F32)
    for fetch in fetches[1:4]:
        fetch.wait()
    token_ids = ids[...]
    token_weight = jnp.zeros((1, tokens), F32)
    for x in range(EXAMPLES):
        token_weight = jnp.where(token_ids == x, loss[0, x], token_weight)
    token_code = (token_ids + 1).astype(F32)
    ready = []
    for k in range(sources):
        scale = jnp.sum(jnp.where(matches[k], weights[...], 0.0), axis=0, keepdims=True)
        scale = scale * token_weight
        placed = jnp.where(ranking[k : k + 1] == slot, hits[k], 0.0)
        slot_scale = jnp.sum(placed * scale, axis=1, keepdims=True)
        code = jnp.sum(placed * token_code, axis=1, keepdims=True)
        ready.append((placed.astype(BF16), slot_scale, code))
    fetches[4].wait()
    for k in range(sources):
        placed, slot_scale, code = ready[k]
        rows = jnp.dot(placed, grad[...], preferred_element_type=F32)
        rows = (rows * slot_scale).astype(BF16)
        if k == 0:
            own[...] = rows
            own_code[...] = jnp.broadcast_to(code, (cap, LANES))
        else:
            gives[k - 1][:, :width] = rows
            gives[k - 1][:, width:] = jnp.broadcast_to(code, (cap, LANES)).astype(BF16)


def cut(sources, n_dp, pad, hidden, *outs):
    me, rank = lax.axis_index("expert"), lax.axis_index("dp")
    near = n_dp // FAR
    bits = near.bit_length() - 1
    ff = hidden.shape[2]
    rows = ff // n_dp
    mine, here = rank // near, lax.rem(rank, near)
    column = iota((1, near * pad), 1)
    wanted = jnp.full((1, near * pad), -ff, jnp.int32)
    for p in range(near):
        inside = (column >= p * pad) & (column < p * pad + rows)
        wanted = jnp.where(
            inside, (here ^ reversed_bits(p, bits)) * rows + column - p * pad, wanted
        )
    unit = iota((ff, near * pad), 0)
    acts = [hidden[lax.rem(me + j, sources)] for j in range(sources)]
    acts = jnp.concatenate(acts, axis=0)
    for k in range(FAR):
        pick = jnp.where(unit == wanted + (mine ^ k) * (near * rows), 1.0, 0.0).astype(BF16)
        outs[k][...] = jnp.dot(acts, pick, preferred_element_type=F32).astype(BF16)


def meet(sources, hidden, own, own_code, turned, *refs):
    takes, cuts = refs[: sources - 1], refs[sources - 1 : sources - 1 + FAR]
    squares, outs = refs[-FAR - 1], refs[-FAR:]
    me = lax.axis_index("expert")
    cap, width = own.shape
    across = cuts[0].shape[1]
    acts = jnp.concatenate([hidden[lax.rem(me + j, sources)] for j in range(sources)], axis=0)
    cot = jnp.concatenate([own[...]] + [t[:, :width] for t in takes], axis=0)
    member = membership(own_code, takes, width)
    last = (((1,), (1,)), ((), ()))
    left = lax.dot_general(acts, acts, last, preferred_element_type=F32)
    right = lax.dot_general(cot, cot, last, preferred_element_type=F32)
    one_hot = member.astype(BF16)
    alike = lax.dot_general(one_hot, one_hot, last, preferred_element_type=F32)
    per_slot = jnp.sum(left * right * alike, axis=1, keepdims=True)
    squares[...] = jnp.sum(per_slot * member, axis=0, keepdims=True)
    for k in range(FAR):
        for j in range(1, sources):
            part = slice((j - 1) * cap, j * cap)
            outs[k][part, :width] = takes[j - 1][:, :width]
            outs[k][part, width : width + across] = cuts[k][j * cap : (j + 1) * cap]
            if j > 1:
                outs[k][part, width + across :] = jnp.zeros(
                    (cap, outs[k].shape[1] - width - across), BF16
                )
        outs[k][:cap, width + across : width + 2 * across] = cuts[k][:cap]
    outs[1][:cap, width + 2 * across : 2 * width + 2 * across] = own[...]
    outs[1][:cap, 2 * width + 2 * across :] = turned[...]


def membership(own_code, takes, width):
    code = jnp.concatenate(
        [own_code[...]] + [t[:, width:].astype(F32) for t in takes], axis=0
    )
    lane = iota(code.shape, 1).astype(F32)
    return jnp.where((code == lane) & (code > 0.0), 1.0, 0.0)


def weigh(sources, scale, own_code, *refs):
    takes = refs[: sources - 1]
    squares, out = refs[sources - 1 : -1], refs[-1]
    cap = own_code.shape[0]
    total = squares[0][...]
    for s in squares[1:]:
        total = total + s[...]
    clip = 1.0 / jnp.maximum(jnp.sqrt(total / scale), 1.0)
    member = membership(own_code, takes, takes[0].shape[1] - LANES)
    weight = jnp.sum(member * clip, axis=1, keepdims=True) / EXAMPLES
    diagonal = iota((cap, LANES), 0) == iota((cap, LANES), 1)
    for j in range(sources):
        here = jnp.where(diagonal, weight[j * cap : (j + 1) * cap], 0.0)
        out[j : j + 1] = jnp.sum(here, axis=0, keepdims=True)


def product(sources, rows, pad, *refs):
    straight, turned = refs[:2]
    rests, weights = refs[2 : 2 + FAR], refs[2 + FAR : 2 + 2 * FAR]
    keep, give, cots, units = refs[2 + 2 * FAR :]
    cap, width = straight.shape
    across = units.shape[1]
    first = width + 2 * across
    owns = [
        straight,
        rests[1].at[:cap, first : first + width],
        turned,
        rests[1].at[:cap, first + width :],
    ]
    slots = sources * cap
    diagonal = iota((cap, LANES), 0) == iota((cap, LANES), 1)
    for k in range(FAR):
        for j in range(sources):
            at = slice(k * slots + j * cap, k * slots + (j + 1) * cap)
            weight = jnp.where(diagonal, weights[k][j : j + 1], 0.0)
            weight = jnp.sum(weight, axis=1, keepdims=True)
            part = slice((j - 1) * cap, j * cap)
            cot = owns[k][...] if j == 0 else rests[k][part, :width]
            cots[at] = (weight * cot.astype(F32)).astype(BF16)
            if j == 0:
                units[at] = rests[k][:cap, width + across : width + 2 * across]
            else:
                units[at] = rests[k][part, width : width + across]
    half = keep.shape[0]
    pieces = width // LANES
    part = lax.dot_general(
        units[...], cots[...], (((0,), (0,)), ((), ())), preferred_element_type=F32
    )
    for p in range(2 * half):
        out = keep if p < half else give
        for j in range(pieces):
            out[p % half, pl.ds(j, rows, stride=pieces), :] = part[
                p * pad : p * pad + rows, j * LANES : (j + 1) * LANES
            ]


def call(body, outs, args, fetched=False, scratch=(), limit=32):
    vmem = pl.BlockSpec(memory_space=pltpu.VMEM)
    hbm = pl.BlockSpec(memory_space=pltpu.HBM)
    return pl.pallas_call(
        body,
        out_shape=tuple(outs),
        in_specs=[hbm if fetched else vmem] * len(args),
        out_specs=tuple([vmem] * len(outs)),
        scratch_shapes=list(scratch),
        compiler_params=pltpu.CompilerParams(vmem_limit_bytes=limit * 1024 * 1024),
        cost_estimate=pl.CostEstimate(flops=1, bytes_accessed=1, transcendentals=0),
    )(*args)


def shards(grad_out, routes, route_weight, example_ids, example_weight, hidden):
    sources = lax.axis_size("expert")
    n_dp = lax.axis_size("dp")
    near = n_dp // FAR
    tokens, width = grad_out.shape
    top = routes.shape[1]
    cap, ff = hidden.shape[3], hidden.shape[4]
    rows = ff // n_dp
    pad = -(-rows // 16) * 16
    while near * pad * 2 % LANES:
        pad += 16
    across = near * pad
    slots = sources * cap
    acts = hidden.reshape(sources, cap, ff)
    shape = jax.ShapeDtypeStruct

    def over_experts(array, k):
        return lax.ppermute(
            array, "expert", [(s, (s - k) % sources) for s in range(sources)]
        )

    def over_far(array, k):
        return lax.ppermute(array, "dp", [(i, i ^ (k * near)) for i in range(n_dp)])

    own, own_code, *gives = call(
        lambda *refs: build(sources, cap, *refs),
        [shape((cap, width), BF16), shape((cap, LANES), F32)]
        + [shape((cap, width + LANES), BF16)] * (sources - 1),
        (routes.T, route_weight.T, example_ids, example_weight, grad_out),
        fetched=True,
        limit=60,
        scratch=(
            pltpu.VMEM((top, tokens), jnp.int32),
            pltpu.VMEM((top, tokens), F32),
            pltpu.VMEM((1, tokens), jnp.int32),
            pltpu.SMEM((1, EXAMPLES), F32),
            pltpu.VMEM((tokens, width), BF16),
            pltpu.SemaphoreType.DMA((5,)),
        ),
    )
    takes = [over_experts(g, k + 1) for k, g in enumerate(gives)]
    turned = over_far(own, 2)

    cuts = call(
        lambda *refs: cut(sources, n_dp, pad, *refs),
        [shape((slots, across), BF16)] * FAR,
        (acts,),
    )
    squares, *rests = call(
        lambda *refs: meet(sources, *refs),
        [shape((1, LANES), F32)]
        + [
            shape((slots - cap, width + 2 * across + (2 * width if k == 1 else 0)), BF16)
            for k in range(FAR)
        ],
        (acts, own, own_code, turned, *takes, *cuts),
    )
    all_squares = [squares] + [over_experts(squares, k) for k in range(1, sources)]
    rests = [rests[0]] + [over_far(rests[k], k) for k in range(1, FAR)]
    (weight,) = call(
        lambda *refs: weigh(sources, ff * width, *refs),
        [shape((-(-sources // 8) * 8, LANES), F32)],
        (own_code, *takes, *all_squares),
    )
    weights = [weight] + [over_far(weight, k) for k in range(1, FAR)]

    keep, give = call(
        lambda *refs: product(sources, rows, pad, *refs),
        [shape((near // 2, rows * (width // LANES), LANES), F32)] * 2,
        (own, turned, *rests, *weights),
        scratch=(
            pltpu.VMEM((FAR * slots, width), BF16),
            pltpu.VMEM((FAR * slots, across), BF16),
        ),
    )
    bit = 1
    while True:
        part = keep + lax.ppermute(give, "dp", [(i, i ^ bit) for i in range(n_dp)])
        half = part.shape[0] // 2
        if half == 0:
            break
        keep, give, bit = part[:half], part[half:], bit * 2
    return part.reshape(rows, 1, width)


def solution(mesh):
    placed = (
        P(("dp", "expert"), None),
        P(("dp", "expert"), None),
        P(("dp", "expert"), None),
        P("dp", "expert"),
        P("dp", None),
        P("dp", "expert", None, None, None),
    )
    return jax.shard_map(
        shards, mesh=mesh, in_specs=placed, out_specs=P("dp", "expert", None), check_vma=False
    )
```

time: 47.4 us -> 44 us (0.928)
  starting transfers between devices: 20.9 us -> 15.7 us
  waiting for transfers between devices: 19.7 us -> 23.5 us
  local copies, waits for them, and re-layouts: 3.13 us -> 0.02 us
  Pallas kernels: 2.54 us -> 3.76 us
    ppermute x9 -> x7, waiting for transfers between devices: 8.1 us -> 13.6 us  [over_far(): return lax.ppermute(array, 'dp', [(i, i ^ k * near) for i in range(n_dp)])]
    ppermute x9 -> x7, starting transfers between devices: 14.5 us -> 10.6 us  [over_far(): return lax.ppermute(array, 'dp', [(i, i ^ k * near) for i in range(n_dp)])]
    unnamed x12 -> x6, local copies, waits for them, and re-layouts: 3.12 us -> 0.01 us
    ppermute x2, waiting for transfers between devices: 4.85 us -> 3.07 us  [over_experts(): lax.ppermute(array, 'expert', [(s, (s - k) % sources) for s in range(sour...]
    ppermute x2, starting transfers between devices: 4.82 us -> 3.5 us  [over_experts(): lax.ppermute(array, 'expert', [(s, (s - k) % sources) for s in range(sour...]
    pallas_call x5, Pallas kernels: 2.54 us -> 3.76 us  [call(): pl.pallas_call(body, out_shape=tuple(outs), in_specs=[hbm if fetched else...]
  transfers between devices with their start and end apart: 13 -> 11, of which waited for: 8 -> 6; matrix products, arithmetic and copies ran while one was open for 0% -> 0% of each run, Pallas kernels for 1% -> 1%
where the time goes in v3:
time: 44 us; the launch traced here: 43.8 us
  waiting for transfers between devices  23.5 us (53%)
  starting transfers between devices  15.7 us (36%)
  Pallas kernels  3.76 us (9%)
  other arithmetic  0.75 us (2%)
    ppermute x7, waiting for transfers between devices, over_far(): return lax.ppermute(array, 'dp', [(i, i ^ k * near) for i in range(n_dp)])  13.6 us
    ppermute x7, starting transfers between devices, over_far(): return lax.ppermute(array, 'dp', [(i, i ^ k * near) for i in range(n_dp)])  10.6 us
    ppermute x2, waiting for transfers between devices, shards(): part = keep + lax.ppermute(give, 'dp', [(i, i ^ bit) for i in range(n_dp)])  6.77 us
    pallas_call x5, Pallas kernels, call(): pl.pallas_call(body, out_shape=tuple(outs), in_specs=[hbm if fetched else...  3.76 us
    ppermute x2, starting transfers between devices, over_experts(): lax.ppermute(array, 'expert', [(s, (s - k) % sources) for s in range(sour...  3.5 us
    ppermute x2, waiting for transfers between devices, over_experts(): lax.ppermute(array, 'expert', [(s, (s - k) % sources) for s in range(sour...  3.07 us
    ppermute x2, starting transfers between devices, shards(): part = keep + lax.ppermute(give, 'dp', [(i, i ^ bit) for i in range(n_dp)])  1.62 us
  transfers between devices with their start and end apart: 11, of which 6 were waited for; matrix products, arithmetic and copies ran while one was open for 0% of the time, Pallas kernels for 1%

profile of v3, /device:TPU:0, one launch (start us, length us, event | category | flops | bytes accessed | tf_op | source)
XLA Modules:
  0.0 43.8 jit_solution(692247556208587173)
XLA Ops:
  0.0 0.0 copy-start
  0.0 2.1 %shard_map.64 = (bf16[48,1024]{1,0:T(8,128)(2,1)}, f32[48,128]{1,0:T(8,128)}, bf16[48,1152]{1,0:T(8,128)(2,1)}) custom-call(s32[6,256]{1,0:T(8,128)} %bitcast.6, f32[6,256]{1,0:T(8,128)} %bitcast.7, s32[1,256]{1,0:T(1,128)} %refs_2_.1, f32[1,8]{1,0:T(1,128)} %refs_3_.1, bf16[256,1024]{1,0:T(8,128)(2,1)} %refs_4_.1), custom_call_target="tpu_custom_call" | custom-call | flops 1 | bytes 1 | tf_op jit(solution)/shard_map/pallas_call | solution.py:197
  2.2 0.0 copy-start.1
  2.2 3.0 %collective-permute-start.1 = (bf16[48,1152]{1,0:T(8,128)(2,1)}, bf16[48,1152]{1,0:T(8,128)(2,1)S(1)}, u32[]{:S(2)}, u32[]{:S(2)}) collective-permute-start(bf16[48,1152]{1,0:T(8,128)(2,1)} %get-tuple-element.21), channel_id=1, source_target_pairs={{0,1},{1,0},{2,3},{3,2},{4,5},{5,4},{6,7},{7,6},{8,9},{9,8},{10,11... | collective-permute-start | bytes 331784 | tf_op jit(solution)/shard_map/ppermute | solution.py:225
  5.2 2.6 %collective-permute-start = (bf16[48,1024]{1,0:T(8,128)(2,1)}, bf16[48,1024]{1,0:T(8,128)(2,1)S(1)}, u32[]{:S(2)}, u32[]{:S(2)}) collective-permute-start(bf16[48,1024]{1,0:T(8,128)(2,1)} %get-tuple-element.19.refs_1_.refs_0_), channel_id=1, source_target_pairs={{0,16},{2,18},{4,20},{6,22},{8,24},{10,26},{12,28},{14,30},{16,0},... | collective-permute-start | bytes 294920 | tf_op jit(solution)/shard_map/ppermute | solution.py:230
  7.8 0.0 copy-done
  7.8 0.0 copy-start.2
  7.8 0.4 shard_map.65
  8.2 4.5 %collective-permute-done.refs_3_.refs_1_ = bf16[48,1024]{1,0:T(8,128)(2,1)S(1)} collective-permute-done((bf16[48,1024]{1,0:T(8,128)(2,1)}, bf16[48,1024]{1,0:T(8,128)(2,1)S(1)}, u32[]{:S(2)}, u32[]{:S(2)}) %collective-permute-start) | collective-permute-done | bytes 98336 | tf_op jit(solution)/shard_map/ppermute | solution.py:230
  12.7 0.0 collective-permute-done.1.refs_4_.refs_1_
  12.7 0.0 copy-done.1
  12.7 0.0 copy-done.2
  12.7 0.3 shard_map.66
  13.0 0.8 %collective-permute-start.2 = (bf16[48,3456]{1,0:T(8,128)(2,1)S(1)}, bf16[48,3456]{1,0:T(8,128)(2,1)S(1)}, u32[]{:S(2)}, u32[]{:S(2)}) collective-permute-start(bf16[48,3456]{1,0:T(8,128)(2,1)S(1)} %get-tuple-element.27), channel_id=1, source_target_pairs={{0,8},{2,10},{4,12},{6,14},{8,0},{10,2},{12,4},{14,6},{16,24},{18,... | collective-permute-start | bytes 995336 | tf_op jit(solution)/shard_map/ppermute | solution.py:230
  13.9 3.3 %collective-permute-start.3 = (bf16[48,1408]{1,0:T(8,128)(2,1)S(1)}, bf16[48,1408]{1,0:T(8,128)(2,1)S(1)}, u32[]{:S(2)}, u32[]{:S(2)}) collective-permute-start(bf16[48,1408]{1,0:T(8,128)(2,1)S(1)} %get-tuple-element.28), channel_id=1, source_target_pairs={{0,16},{2,18},{4,20},{6,22},{8,24},{10,26},{12,28},{14,30},{16,0},... | collective-permute-start | bytes 405512 | tf_op jit(solution)/shard_map/ppermute | solution.py:230
  17.2 0.3 collective-permute-start.4
  17.5 0.5 %collective-permute-start.5 = (f32[1,128]{1,0:T(1,128)S(1)}, f32[1,128]{1,0:T(1,128)S(1)}, u32[]{:S(2)}, u32[]{:S(2)}) collective-permute-start(f32[1,128]{1,0:T(1,128)S(1)} %get-tuple-element.30.refs_2_), channel_id=1, source_target_pairs={{0,1},{1,0},{2,3},{3,2},{4,5},{5,4},{6,7},{7,6},{8,9},{9,8},{10,11... | collective-permute-start | bytes 1544 | tf_op jit(solution)/shard_map/ppermute | solution.py:225
  18.0 3.1 %collective-permute-done.5.refs_3_ = f32[1,128]{1,0:T(1,128)S(1)} collective-permute-done((f32[1,128]{1,0:T(1,128)S(1)}, f32[1,128]{1,0:T(1,128)S(1)}, u32[]{:S(2)}, u32[]{:S(2)}) %collective-permute-start.5) | collective-permute-done | bytes 544 | tf_op jit(solution)/shard_map/ppermute | solution.py:225
  21.0 0.1 shard_map.67.refs_6_
  21.1 3.6 %collective-permute-start.8 = (f32[8,128]{1,0:T(8,128)S(1)}, f32[8,128]{1,0:T(8,128)S(1)}, u32[]{:S(2)}, u32[]{:S(2)}) collective-permute-start(f32[8,128]{1,0:T(8,128)S(1)} %shard_map.67.refs_6_), channel_id=1, source_target_pairs={{0,24},{2,26},{4,28},{6,30},{8,16},{10,18},{12,20},{14,22},{16,8},... | collective-permute-start | bytes 12296 | tf_op jit(solution)/shard_map/ppermute | solution.py:230
  24.7 0.0 collective-permute-start.7
  24.7 5.6 %collective-permute-done.8.refs_9_ = f32[8,128]{1,0:T(8,128)S(1)} collective-permute-done((f32[8,128]{1,0:T(8,128)S(1)}, f32[8,128]{1,0:T(8,128)S(1)}, u32[]{:S(2)}, u32[]{:S(2)}) %collective-permute-start.8) | collective-permute-done | bytes 4128 | tf_op jit(solution)/shard_map/ppermute | solution.py:230
  30.3 0.0 collective-permute-start.6
  30.3 0.0 collective-permute-done.7.refs_8_
  30.3 3.6 %collective-permute-done.6.refs_7_ = f32[8,128]{1,0:T(8,128)S(1)} collective-permute-done((f32[8,128]{1,0:T(8,128)S(1)}, f32[8,128]{1,0:T(8,128)S(1)}, u32[]{:S(2)}, u32[]{:S(2)}) %collective-permute-start.6) | collective-permute-done | bytes 4128 | tf_op jit(solution)/shard_map/ppermute | solution.py:230
  33.9 0.0 collective-permute-done.3.refs_4_
  33.9 0.0 collective-permute-done.4.refs_5_
  33.9 0.0 collective-permute-done.2.refs_3_
  33.9 0.8 %shard_map.68 = (f32[2,352,128]{2,1,0:T(8,128)S(1)}, f32[2,352,128]{2,1,0:T(8,128)S(1)}) custom-call(bf16[48,1024]{1,0:T(8,128)(2,1)S(1)} %copy-done.1, bf16[48,1024]{1,0:T(8,128)(2,1)S(1)} %collective-permute-done.refs_3_.refs_1_, bf16[48,1408]{1,0:T(8,128)(2,1)S(1)} %get-tuple-element.26.refs_2_, bf16[48,3456]{1,0:T(8,128)(2,1)S(1)} %collective-permute-done.2.refs_3_, ...), custom_call_target="tpu_custom_call" | custom-call | flops 1 | bytes 1 | tf_op jit(solution)/shard_map/pallas_call | solution.py:197
  34.7 0.1 collective-permute-start.9
  34.7 1.7 %collective-permute-done.9 = f32[2,352,128]{2,1,0:T(8,128)S(1)} collective-permute-done((f32[2,352,128]{2,1,0:T(8,128)S(1)}, f32[2,352,128]{2,1,0:T(8,128)S(1)}, u32[]{:S(2)}, u32[]{:S(2)}) %collective-permute-start.9) | collective-permute-done | bytes 360480 | tf_op jit(solution)/shard_map/ppermute | solution.py:285
  36.4 0.1 add.6
  36.5 1.6 %collective-permute-start.10 = (f32[1,352,128]{2,1,0:T(8,128)S(1)}, f32[1,352,128]{2,1,0:T(8,128)S(1)}, u32[]{:S(2)}, u32[]{:S(2)}) collective-permute-start(f32[1,352,128]{2,1,0:T(8,128)S(1)} %slice.9), channel_id=1, source_target_pairs={{0,4},{2,6},{4,0},{6,2},{8,12},{10,14},{12,8},{14,10},{16,20},{18,... | collective-permute-start | bytes 540680 | tf_op jit(solution)/shard_map/ppermute | solution.py:285
  38.0 5.1 %collective-permute-done.10 = f32[1,352,128]{2,1,0:T(8,128)S(1)} collective-permute-done((f32[1,352,128]{2,1,0:T(8,128)S(1)}, f32[1,352,128]{2,1,0:T(8,128)S(1)}, u32[]{:S(2)}, u32[]{:S(2)}) %collective-permute-start.10) | collective-permute-done | bytes 180256 | tf_op jit(solution)/shard_map/ppermute | solution.py:285
  43.1 0.7 %slice_add_fusion = f32[1,352,128]{2,1,0:T(8,128)} fusion(f32[1,352,128]{2,1,0:T(8,128)S(1)} %collective-permute-done.10, f32[2,352,128]{2,1,0:T(8,128)S(1)} %add.6), kind=kLoop, calls=%fused_computation | loop fusion | flops 45056 | bytes 540672 | tf_op jit(solution)/shard_map/add | solution.py:285
  (1 shorter events, 0.0 us)
Async XLA Ops:
  0.0 7.8 %copy-start = (bf16[1,1,2,48,704]{4,3,2,1,0:T(8,128)(2,1)S(1)}, bf16[1,1,2,48,704]{4,3,2,1,0:T(8,128)(2,1)}, u32[]{:S(2)}) copy-start(bf16[1,1,2,48,704]{4,3,2,1,0:T(8,128)(2,1)} %param.11) | copy-start | bytes 405508
  2.2 10.5 %copy-start.1 = (bf16[48,1024]{1,0:T(8,128)(2,1)S(1)}, bf16[48,1024]{1,0:T(8,128)(2,1)}, u32[]{:S(2)}) copy-start(bf16[48,1024]{1,0:T(8,128)(2,1)} %get-tuple-element.19.refs_1_.refs_0_) | copy-start | bytes 294916
  2.2 10.5 %collective-permute-start.1 = (bf16[48,1152]{1,0:T(8,128)(2,1)}, bf16[48,1152]{1,0:T(8,128)(2,1)S(1)}, u32[]{:S(2)}, u32[]{:S(2)}) collective-permute-start(bf16[48,1152]{1,0:T(8,128)(2,1)} %get-tuple-element.21), channel_id=1, source_target_pairs={{0,1},{1,0},{2,3},{3,2},{4,5},{5,4},{6,7},{7,6},{8,9},{9,8},{10,11... | collective-permute-start | bytes 331784 | tf_op jit(solution)/shard_map/ppermute | solution.py:225
  5.2 7.5 %collective-permute-start = (bf16[48,1024]{1,0:T(8,128)(2,1)}, bf16[48,1024]{1,0:T(8,128)(2,1)S(1)}, u32[]{:S(2)}, u32[]{:S(2)}) collective-permute-start(bf16[48,1024]{1,0:T(8,128)(2,1)} %get-tuple-element.19.refs_1_.refs_0_), channel_id=1, source_target_pairs={{0,16},{2,18},{4,20},{6,22},{8,24},{10,26},{12,28},{14,30},{16,0},... | collective-permute-start | bytes 294920 | tf_op jit(solution)/shard_map/ppermute | solution.py:230
  7.8 4.9 %copy-start.2 = (f32[48,128]{1,0:T(8,128)S(1)}, f32[48,128]{1,0:T(8,128)}, u32[]{:S(2)}) copy-start(f32[48,128]{1,0:T(8,128)} %get-tuple-element.20.refs_2_.refs_0_) | copy-start | bytes 73732
  13.0 20.8 %collective-permute-start.2 = (bf16[48,3456]{1,0:T(8,128)(2,1)S(1)}, bf16[48,3456]{1,0:T(8,128)(2,1)S(1)}, u32[]{:S(2)}, u32[]{:S(2)}) collective-permute-start(bf16[48,3456]{1,0:T(8,128)(2,1)S(1)} %get-tuple-element.27), channel_id=1, source_target_pairs={{0,8},{2,10},{4,12},{6,14},{8,0},{10,2},{12,4},{14,6},{16,24},{18,... | collective-permute-start | bytes 995336 | tf_op jit(solution)/shard_map/ppermute | solution.py:230
  13.9 20.0 %collective-permute-start.3 = (bf16[48,1408]{1,0:T(8,128)(2,1)S(1)}, bf16[48,1408]{1,0:T(8,128)(2,1)S(1)}, u32[]{:S(2)}, u32[]{:S(2)}) collective-permute-start(bf16[48,1408]{1,0:T(8,128)(2,1)S(1)} %get-tuple-element.28), channel_id=1, source_target_pairs={{0,16},{2,18},{4,20},{6,22},{8,24},{10,26},{12,28},{14,30},{16,0},... | collective-permute-start | bytes 405512 | tf_op jit(solution)/shard_map/ppermute | solution.py:230
  17.2 16.7 %collective-permute-start.4 = (bf16[48,1408]{1,0:T(8,128)(2,1)S(1)}, bf16[48,1408]{1,0:T(8,128)(2,1)S(1)}, u32[]{:S(2)}, u32[]{:S(2)}) collective-permute-start(bf16[48,1408]{1,0:T(8,128)(2,1)S(1)} %get-tuple-element.29), channel_id=1, source_target_pairs={{0,24},{2,26},{4,28},{6,30},{8,16},{10,18},{12,20},{14,22},{16,8},... | collective-permute-start | bytes 405512 | tf_op jit(solution)/shard_map/ppermute | solution.py:230
  17.5 3.5 %collective-permute-start.5 = (f32[1,128]{1,0:T(1,128)S(1)}, f32[1,128]{1,0:T(1,128)S(1)}, u32[]{:S(2)}, u32[]{:S(2)}) collective-permute-start(f32[1,128]{1,0:T(1,128)S(1)} %get-tuple-element.30.refs_2_), channel_id=1, source_target_pairs={{0,1},{1,0},{2,3},{3,2},{4,5},{5,4},{6,7},{7,6},{8,9},{9,8},{10,11... | collective-permute-start | bytes 1544 | tf_op jit(solution)/shard_map/ppermute | solution.py:225
  21.1 9.1 %collective-permute-start.8 = (f32[8,128]{1,0:T(8,128)S(1)}, f32[8,128]{1,0:T(8,128)S(1)}, u32[]{:S(2)}, u32[]{:S(2)}) collective-permute-start(f32[8,128]{1,0:T(8,128)S(1)} %shard_map.67.refs_6_), channel_id=1, source_target_pairs={{0,24},{2,26},{4,28},{6,30},{8,16},{10,18},{12,20},{14,22},{16,8},... | collective-permute-start | bytes 12296 | tf_op jit(solution)/shard_map/ppermute | solution.py:230
  24.7 5.6 %collective-permute-start.7 = (f32[8,128]{1,0:T(8,128)S(1)}, f32[8,128]{1,0:T(8,128)S(1)}, u32[]{:S(2)}, u32[]{:S(2)}) collective-permute-start(f32[8,128]{1,0:T(8,128)S(1)} %shard_map.67.refs_6_), channel_id=1, source_target_pairs={{0,16},{2,18},{4,20},{6,22},{8,24},{10,26},{12,28},{14,30},{16,0},... | collective-permute-start | bytes 12296 | tf_op jit(solution)/shard_map/ppermute | solution.py:230
  30.3 3.6 %collective-permute-start.6 = (f32[8,128]{1,0:T(8,128)S(1)}, f32[8,128]{1,0:T(8,128)S(1)}, u32[]{:S(2)}, u32[]{:S(2)}) collective-permute-start(f32[8,128]{1,0:T(8,128)S(1)} %shard_map.67.refs_6_), channel_id=1, source_target_pairs={{0,8},{2,10},{4,12},{6,14},{8,0},{10,2},{12,4},{14,6},{16,24},{18,... | collective-permute-start | bytes 12296 | tf_op jit(solution)/shard_map/ppermute | solution.py:230
  34.7 1.7 %collective-permute-start.9 = (f32[2,352,128]{2,1,0:T(8,128)S(1)}, f32[2,352,128]{2,1,0:T(8,128)S(1)}, u32[]{:S(2)}, u32[]{:S(2)}) collective-permute-start(f32[2,352,128]{2,1,0:T(8,128)S(1)} %get-tuple-element.32), channel_id=1, source_target_pairs={{0,2},{2,0},{4,6},{6,4},{8,10},{10,8},{12,14},{14,12},{16,18},{18,... | collective-permute-start | bytes 1081352 | tf_op jit(solution)/shard_map/ppermute | solution.py:285
  36.5 6.7 %collective-permute-start.10 = (f32[1,352,128]{2,1,0:T(8,128)S(1)}, f32[1,352,128]{2,1,0:T(8,128)S(1)}, u32[]{:S(2)}, u32[]{:S(2)}) collective-permute-start(f32[1,352,128]{2,1,0:T(8,128)S(1)} %slice.9), channel_id=1, source_target_pairs={{0,4},{2,6},{4,0},{6,2},{8,12},{10,14},{12,8},{14,10},{16,20},{18,... | collective-permute-start | bytes 540680 | tf_op jit(solution)/shard_map/ppermute | solution.py:285

commit v4 on v3

v4 whole, which is shorter than its diff:
```python
import jax
import jax.numpy as jnp
from jax import lax
from jax.experimental import pallas as pl
from jax.experimental.pallas import tpu as pltpu
from jax.sharding import PartitionSpec as P

EXAMPLES = 8
FAR = 4
LANES = 128
BF16 = jnp.bfloat16
F32 = jnp.float32


def iota(shape, axis):
    return lax.broadcasted_iota(jnp.int32, shape, axis)


def reversed_bits(p, count):
    return int(format(p, "b").zfill(count)[::-1], 2) if count else 0


def build(sources, cap, n_dp, pad, routes_at, weights_at, ids_at, loss_at, grad_at, hidden_at, *refs):
    own, own_code, *gives = refs[: sources + 1]
    parcels = refs[sources + 1 : sources + 1 + FAR]
    routes, weights, ids, loss, grad, hidden, sems = refs[sources + 1 + FAR :]
    fetches = [
        pltpu.make_async_copy(source, target, sems.at[i])
        for i, (source, target) in enumerate(
            [
                (routes_at, routes),
                (ids_at, ids),
                (loss_at, loss),
                (weights_at, weights),
                (hidden_at, hidden),
                (grad_at, grad),
            ]
        )
    ]
    for fetch in fetches:
        fetch.start()
    me = lax.axis_index("expert")
    tokens, width = grad.shape
    before = (iota((tokens, tokens), 0) < iota((tokens, tokens), 1)).astype(F32).astype(BF16)
    slot = iota((cap, tokens), 0).astype(F32)
    fetches[0].wait()
    matches = [routes[...] == lax.rem(me + (sources - k), sources) for k in range(sources)]
    hits = [jnp.sum(jnp.where(m, 1.0, 0.0), axis=0, keepdims=True) for m in matches]
    blank = -(-sources // 8) * 8 - sources
    routed = jnp.concatenate(hits + [jnp.zeros((1, tokens), F32)] * blank, axis=0)
    ranking = jnp.dot(routed.astype(BF16), before, preferred_element_type=F32)
    for fetch in fetches[1:4]:
        fetch.wait()
    token_ids = ids[...]
    token_weight = jnp.zeros((1, tokens), F32)
    for x in range(EXAMPLES):
        token_weight = jnp.where(token_ids == x, loss[0, x], token_weight)
    token_code = (token_ids + 1).astype(F32)
    ready = []
    for k in range(sources):
        scale = jnp.sum(jnp.where(matches[k], weights[...], 0.0), axis=0, keepdims=True)
        scale = scale * token_weight
        placed = jnp.where(ranking[k : k + 1] == slot, hits[k], 0.0)
        slot_scale = jnp.sum(placed * scale, axis=1, keepdims=True)
        code = jnp.sum(placed * token_code, axis=1, keepdims=True)
        ready.append((placed.astype(BF16), slot_scale, code))
    fetches[4].wait()
    cut_hidden(sources, n_dp, pad, width, hidden, parcels)
    fetches[5].wait()
    for k in range(sources):
        placed, slot_scale, code = ready[k]
        rows = jnp.dot(placed, grad[...], preferred_element_type=F32)
        rows = (rows * slot_scale).astype(BF16)
        if k == 0:
            own[...] = rows
            own_code[...] = jnp.broadcast_to(code, (cap, LANES))
            parcels[1][:, :width] = rows
            parcels[2][:, :width] = rows
        else:
            gives[k - 1][:, :width] = rows
            gives[k - 1][:, width:] = jnp.broadcast_to(code, (cap, LANES)).astype(BF16)


def cut_hidden(sources, n_dp, pad, width, hidden, parcels):
    me, rank = lax.axis_index("expert"), lax.axis_index("dp")
    near = n_dp // FAR
    bits = near.bit_length() - 1
    cap, ff = hidden.shape[1:]
    rows = ff // n_dp
    mine, here = rank // near, lax.rem(rank, near)
    column = iota((1, near * pad), 1)
    wanted = jnp.full((1, near * pad), -ff, jnp.int32)
    for p in range(near):
        inside = (column >= p * pad) & (column < p * pad + rows)
        wanted = jnp.where(
            inside, (here ^ reversed_bits(p, bits)) * rows + column - p * pad, wanted
        )
    unit = iota((ff, near * pad), 0)
    acts = [hidden[lax.rem(me + j, sources)] for j in range(sources)]
    acts = jnp.concatenate(acts, axis=0)
    for k in range(FAR):
        pick = jnp.where(unit == wanted + (mine ^ k) * (near * rows), 1.0, 0.0).astype(BF16)
        units = jnp.dot(acts, pick, preferred_element_type=F32).astype(BF16)
        first = width if k in (1, 2) else 0
        for j in range(sources):
            at = slice(first + j * near * pad, first + (j + 1) * near * pad)
            parcels[k][:, at] = units[j * cap : (j + 1) * cap]


def norms(sources, hidden, own, own_code, *refs):
    takes, squares = refs[: sources - 1], refs[sources - 1]
    me = lax.axis_index("expert")
    width = own.shape[1]
    acts = jnp.concatenate([hidden[lax.rem(me + j, sources)] for j in range(sources)], axis=0)
    cot = jnp.concatenate([own[...]] + [t[:, :width] for t in takes], axis=0)
    member = membership(own_code, takes, width)
    last = (((1,), (1,)), ((), ()))
    left = lax.dot_general(acts, acts, last, preferred_element_type=F32)
    right = lax.dot_general(cot, cot, last, preferred_element_type=F32)
    one_hot = member.astype(BF16)
    alike = lax.dot_general(one_hot, one_hot, last, preferred_element_type=F32)
    per_slot = jnp.sum(left * right * alike, axis=1, keepdims=True)
    squares[...] = jnp.sum(per_slot * member, axis=0, keepdims=True)


def membership(own_code, takes, width):
    code = jnp.concatenate(
        [own_code[...]] + [t[:, width:].astype(F32) for t in takes], axis=0
    )
    lane = iota(code.shape, 1).astype(F32)
    return jnp.where((code == lane) & (code > 0.0), 1.0, 0.0)


def scale(sources, count, first, third, own_code, turned, *refs):
    takes, squares = refs[: sources - 1], refs[sources - 1 : 2 * sources - 1]
    rest, longer = refs[2 * sources - 1 :]
    cap = own_code.shape[0]
    width = takes[0].shape[1] - LANES
    total = squares[0][...]
    for s in squares[1:]:
        total = total + s[...]
    clip = 1.0 / jnp.maximum(jnp.sqrt(total / count), 1.0)
    member = membership(own_code, takes, width)
    weight = jnp.sum(member * clip, axis=1, keepdims=True) / EXAMPLES
    own_weight = jnp.broadcast_to(weight[:cap], (cap, LANES))
    high = own_weight.astype(BF16).astype(F32)
    middle = (own_weight - high).astype(BF16).astype(F32)
    low = own_weight - high - middle
    lane = iota((cap, LANES), 1)
    three = jnp.where(lane == 0, high, jnp.where(lane == 1, middle, low)).astype(BF16)
    for j in range(1, sources):
        part = slice((j - 1) * cap, j * cap)
        slot_weight = weight[j * cap : (j + 1) * cap]
        rows = (slot_weight * takes[j - 1][:, :width].astype(F32)).astype(BF16)
        for out in (rest, longer):
            out[part, :width] = rows
            out[part, width : width + LANES] = three
        longer[part, width + LANES :] = turned[:, :width]


def product(sources, rows, pad, *refs):
    own, cut, first, second, third, rest, longer, rest_second, rest_third = refs[:9]
    keep, give, cots, units = refs[9:]
    cap, width = own.shape
    across = units.shape[1]
    slots = sources * cap
    owns = [own, first.at[:, :width], second.at[:, :width], longer.at[:cap, width + LANES :]]
    cuts = [cut, first.at[:, width:], second.at[:, width:], third]
    rests = [rest, longer, rest_second, rest_third]
    for k in range(FAR):
        three = rests[k][:cap, width : width + LANES].astype(F32)
        weight = three[:, 0:1] + three[:, 1:2] + three[:, 2:3]
        at = k * slots
        cots[at : at + cap] = (weight * owns[k][...].astype(F32)).astype(BF16)
        cots[at + cap : at + slots] = rests[k][:, :width]
        for j in range(sources):
            units[at + j * cap : at + (j + 1) * cap] = cuts[k][:, j * across : (j + 1) * across]
    half = keep.shape[0]
    pieces = width // LANES
    part = lax.dot_general(
        units[...], cots[...], (((0,), (0,)), ((), ())), preferred_element_type=F32
    )
    for p in range(2 * half):
        out = keep if p < half else give
        for j in range(pieces):
            out[p % half, pl.ds(j, rows, stride=pieces), :] = part[
                p * pad : p * pad + rows, j * LANES : (j + 1) * LANES
            ]


def call(body, outs, args, fetched=(), scratch=(), limit=32):
    vmem = pl.BlockSpec(memory_space=pltpu.VMEM)
    anywhere = pl.BlockSpec(memory_space=pl.ANY)
    return pl.pallas_call(
        body,
        out_shape=tuple(outs),
        in_specs=[anywhere if i in fetched else vmem for i in range(len(args))],
        out_specs=tuple([vmem] * len(outs)),
        scratch_shapes=list(scratch),
        compiler_params=pltpu.CompilerParams(vmem_limit_bytes=limit * 1024 * 1024),
        cost_estimate=pl.CostEstimate(flops=1, bytes_accessed=1, transcendentals=0),
    )(*args)


def shards(grad_out, routes, route_weight, example_ids, example_weight, hidden):
    sources = lax.axis_size("expert")
    n_dp = lax.axis_size("dp")
    near = n_dp // FAR
    tokens, width = grad_out.shape
    top = routes.shape[1]
    cap, ff = hidden.shape[3], hidden.shape[4]
    rows = ff // n_dp
    pad = -(-rows // 16) * 16
    while near * pad * sources % LANES:
        pad += 16
    across = near * pad
    slots = sources * cap
    acts = hidden.reshape(sources, cap, ff)
    shape = jax.ShapeDtypeStruct

    def over_experts(array, k):
        return lax.ppermute(
            array, "expert", [(s, (s - k) % sources) for s in range(sources)]
        )

    def over_far(array, k):
        return lax.ppermute(array, "dp", [(i, i ^ (k * near)) for i in range(n_dp)])

    own, own_code, *made = call(
        lambda *refs: build(sources, cap, n_dp, pad, *refs),
        [shape((cap, width), BF16), shape((cap, LANES), F32)]
        + [shape((cap, width + LANES), BF16)] * (sources - 1)
        + [
            shape((cap, sources * across + (width if k in (1, 2) else 0)), BF16)
            for k in range(FAR)
        ],
        (routes.T, route_weight.T, example_ids, example_weight, grad_out, acts),
        fetched=range(6),
        limit=60,
        scratch=(
            pltpu.VMEM((top, tokens), jnp.int32),
            pltpu.VMEM((top, tokens), F32),
            pltpu.VMEM((1, tokens), jnp.int32),
            pltpu.SMEM((1, EXAMPLES), F32),
            pltpu.VMEM((tokens, width), BF16),
            pltpu.VMEM((sources, cap, ff), BF16),
            pltpu.SemaphoreType.DMA((6,)),
        ),
    )
    gives, (cut, *parcels) = made[: sources - 1], made[sources - 1 :]
    takes = [over_experts(g, k + 1) for k, g in enumerate(gives)]
    second = over_far(parcels[1], 2)
    first = over_far(parcels[0], 1)
    third = over_far(parcels[2], 3)

    (squares,) = call(
        lambda *refs: norms(sources, *refs),
        [shape((1, LANES), F32)],
        (acts, own, own_code, *takes),
    )
    all_squares = [squares] + [over_experts(squares, k) for k in range(1, sources)]
    rest, longer = call(
        lambda *refs: scale(sources, ff * width, *refs),
        [
            shape((slots - cap, width + LANES), BF16),
            shape((slots - cap, 2 * width + LANES), BF16),
        ],
        (first, third, own_code, second, *takes, *all_squares),
        fetched=(0, 1),
    )
    rests = [rest, over_far(longer, 1), over_far(rest, 2), over_far(rest, 3)]

    keep, give = call(
        lambda *refs: product(sources, rows, pad, *refs),
        [shape((near // 2, rows * (width // LANES), LANES), F32)] * 2,
        (own, cut, first, second, third, *rests),
        scratch=(
            pltpu.VMEM((FAR * slots, width), BF16),
            pltpu.VMEM((FAR * slots, across), BF16),
        ),
    )
    bit = 1
    while True:
        part = keep + lax.ppermute(give, "dp", [(i, i ^ bit) for i in range(n_dp)])
        half = part.shape[0] // 2
        if half == 0:
            break
        keep, give, bit = part[:half], part[half:], bit * 2
    return part.reshape(rows, 1, width)


def solution(mesh):
    placed = (
        P(("dp", "expert"), None),
        P(("dp", "expert"), None),
        P(("dp", "expert"), None),
        P("dp", "expert"),
        P("dp", None),
        P("dp", "expert", None, None, None),
    )
    return jax.shard_map(
        shards, mesh=mesh, in_specs=placed, out_specs=P("dp", "expert", None), check_vma=False
    )
```

time: 44 us -> 39.5 us (0.90)
  waiting for transfers between devices: 23.5 us -> 19.1 us
  local copies, waits for them, and re-layouts: 0.02 us -> 1.65 us
  starting transfers between devices: 15.7 us -> 14.2 us
    ppermute x7 -> x6, waiting for transfers between devices: 13.6 us -> 7.05 us  [over_far(): return lax.ppermute(array, 'dp', [(i, i ^ k * near) for i in range(n_dp)])]
    ppermute x2, waiting for transfers between devices: 3.07 us -> 5.24 us  [over_experts(): lax.ppermute(array, 'expert', [(s, (s - k) % sources) for s in range(sour...]
    unnamed x6 -> x10, local copies, waits for them, and re-layouts: 0.01 us -> 1.64 us
    ppermute x7 -> x6, starting transfers between devices: 10.6 us -> 9.46 us  [over_far(): return lax.ppermute(array, 'dp', [(i, i ^ k * near) for i in range(n_dp)])]
    pallas_call x5 -> x4, Pallas kernels: 3.76 us -> 3.61 us  [call(): pl.pallas_call(body, out_shape=tuple(outs), in_specs=[anywhere if i in fe...]
  transfers between devices with their start and end apart: 11 -> 10, of which waited for: 6 -> 6; matrix products, arithmetic and copies ran while one was open for 0% -> 0% of each run, Pallas kernels for 1% -> 1%
where the time goes in v4:
time: 39.5 us; the launch traced here: 39.3 us
  waiting for transfers between devices  19.1 us (48%)
  starting transfers between devices  14.2 us (36%)
  Pallas kernels  3.61 us (9%)
  local copies, waits for them, and re-layouts  1.65 us (4%)
  other arithmetic  0.75 us (2%)
    ppermute x6, starting transfers between devices, over_far(): return lax.ppermute(array, 'dp', [(i, i ^ k * near) for i in range(n_dp)])  9.46 us
    ppermute x6, waiting for transfers between devices, over_far(): return lax.ppermute(array, 'dp', [(i, i ^ k * near) for i in range(n_dp)])  7.05 us
    ppermute x2, waiting for transfers between devices, shards(): part = keep + lax.ppermute(give, 'dp', [(i, i ^ bit) for i in range(n_dp)])  6.77 us
    ppermute x2, waiting for transfers between devices, over_experts(): lax.ppermute(array, 'expert', [(s, (s - k) % sources) for s in range(sour...  5.24 us
    pallas_call x4, Pallas kernels, call(): pl.pallas_call(body, out_shape=tuple(outs), in_specs=[anywhere if i in fe...  3.61 us
    ppermute x2, starting transfers between devices, over_experts(): lax.ppermute(array, 'expert', [(s, (s - k) % sources) for s in range(sour...  3.1 us
    unnamed x10, local copies, waits for them, and re-layouts  1.64 us
    ppermute x2, starting transfers between devices, shards(): part = keep + lax.ppermute(give, 'dp', [(i, i ^ bit) for i in range(n_dp)])  1.63 us
  transfers between devices with their start and end apart: 10, of which 6 were waited for; matrix products, arithmetic and copies ran while one was open for 0% of the time, Pallas kernels for 1%

profile of v4, /device:TPU:0, one launch (start us, length us, event | category | flops | bytes accessed | tf_op | source)
XLA Modules:
  0.0 39.3 jit_solution(13986575359329399996)
XLA Ops:
  0.0 0.0 copy-start
  0.0 2.5 %shard_map.64 = (bf16[48,1024]{1,0:T(8,128)(2,1)}, f32[48,128]{1,0:T(8,128)}, bf16[48,1152]{1,0:T(8,128)(2,1)}, bf16[48,384]{1,0:T(8,128)(2,1)}, bf16[48,1408]{1...) custom-call(s32[6,256]{1,0:T(8,128)} %bitcast.6, f32[6,256]{1,0:T(8,128)} %bitcast.7, ...), custom_call_target="tpu_custom_call" | custom-call | flops 1 | bytes 1 | tf_op jit(solution)/shard_map/pallas_call | solution.py:194
  2.5 3.1 %collective-permute-start = (bf16[48,1408]{1,0:T(8,128)(2,1)}, bf16[48,1408]{1,0:T(8,128)(2,1)S(1)}, u32[]{:S(2)}, u32[]{:S(2)}) collective-permute-start(bf16[48,1408]{1,0:T(8,128)(2,1)} %get-tuple-element.18), channel_id=1, source_target_pairs={{0,8},{2,10},{4,12},{6,14},{8,0},{10,2},{12,4},{14,6},{16,24},{18,... | collective-permute-start | bytes 405512 | tf_op jit(solution)/shard_map/ppermute | solution.py:227
  5.6 2.6 %collective-permute-start.1 = (bf16[48,1408]{1,0:T(8,128)(2,1)}, bf16[48,1408]{1,0:T(8,128)(2,1)S(1)}, u32[]{:S(2)}, u32[]{:S(2)}) collective-permute-start(bf16[48,1408]{1,0:T(8,128)(2,1)} %get-tuple-element.19), channel_id=1, source_target_pairs={{0,16},{2,18},{4,20},{6,22},{8,24},{10,26},{12,28},{14,30},{16,0},... | collective-permute-start | bytes 405512 | tf_op jit(solution)/shard_map/ppermute | solution.py:227
  8.2 1.5 %collective-permute-start.3 = (bf16[48,1152]{1,0:T(8,128)(2,1)}, bf16[48,1152]{1,0:T(8,128)(2,1)S(1)}, u32[]{:S(2)}, u32[]{:S(2)}) collective-permute-start(bf16[48,1152]{1,0:T(8,128)(2,1)} %get-tuple-element.22), channel_id=1, source_target_pairs={{0,1},{1,0},{2,3},{3,2},{4,5},{5,4},{6,7},{7,6},{8,9},{9,8},{10,11... | collective-permute-start | bytes 331784 | tf_op jit(solution)/shard_map/ppermute | solution.py:222
  9.7 0.2 collective-permute-start.2
  9.9 3.2 %collective-permute-done.3.refs_3_.refs_4_ = bf16[48,1152]{1,0:T(8,128)(2,1)S(1)} collective-permute-done((bf16[48,1152]{1,0:T(8,128)(2,1)}, bf16[48,1152]{1,0:T(8,128)(2,1)S(1)}, u32[]{:S(2)}, u32[]{:S(2)}) %collective-permute-start.3) | collective-permute-done | bytes 110624 | tf_op jit(solution)/shard_map/ppermute | solution.py:222
  13.2 0.0 copy-done
  13.2 0.0 copy-start.1
  13.2 0.9 %copy-done.1 = bf16[48,1024]{1,0:T(8,128)(2,1)S(1)} copy-done((bf16[48,1024]{1,0:T(8,128)(2,1)S(1)}, bf16[48,1024]{1,0:T(8,128)(2,1)}, u32[]{:S(2)}) %copy-start.1) | copy-done | bytes 98328
  14.1 0.0 copy-start.3
  14.1 0.7 %copy-done.3 = f32[48,128]{1,0:T(8,128)S(1)} copy-done((f32[48,128]{1,0:T(8,128)S(1)}, f32[48,128]{1,0:T(8,128)}, u32[]{:S(2)}) %copy-start.3) | copy-done | bytes 24600
  14.8 0.3 shard_map.65.refs_5_
  15.1 0.0 copy-start.2
  15.2 0.0 copy-start.4
  15.2 1.6 %collective-permute-start.4 = (f32[1,128]{1,0:T(1,128)S(1)}, f32[1,128]{1,0:T(1,128)S(1)}, u32[]{:S(2)}, u32[]{:S(2)}) collective-permute-start(f32[1,128]{1,0:T(1,128)S(1)} %shard_map.65.refs_5_), channel_id=1, source_target_pairs={{0,1},{1,0},{2,3},{3,2},{4,5},{5,4},{6,7},{7,6},{8,9},{9,8},{10,11... | collective-permute-start | bytes 1544 | tf_op jit(solution)/shard_map/ppermute | solution.py:222
  16.7 0.0 collective-permute-done.2.refs_1_.refs_4_
  16.8 2.0 %collective-permute-done.4.refs_6_ = f32[1,128]{1,0:T(1,128)S(1)} collective-permute-done((f32[1,128]{1,0:T(1,128)S(1)}, f32[1,128]{1,0:T(1,128)S(1)}, u32[]{:S(2)}, u32[]{:S(2)}) %collective-permute-start.4) | collective-permute-done | bytes 544 | tf_op jit(solution)/shard_map/ppermute | solution.py:222
  18.8 0.0 collective-permute-done.refs_0_.refs_2_
  18.8 0.0 collective-permute-done.1.refs_3_
  18.8 0.1 shard_map.66
  18.9 0.5 %collective-permute-start.5 = (bf16[48,2176]{1,0:T(8,128)(2,1)S(1)}, bf16[48,2176]{1,0:T(8,128)(2,1)S(1)}, u32[]{:S(2)}, u32[]{:S(2)}) collective-permute-start(bf16[48,2176]{1,0:T(8,128)(2,1)S(1)} %get-tuple-element.24), channel_id=1, source_target_pairs={{0,8},{2,10},{4,12},{6,14},{8,0},{10,2},{12,4},{14,6},{16,24},{18,... | collective-permute-start | bytes 626696 | tf_op jit(solution)/shard_map/ppermute | solution.py:227
  19.4 1.3 %collective-permute-start.7 = (bf16[48,1152]{1,0:T(8,128)(2,1)S(1)}, bf16[48,1152]{1,0:T(8,128)(2,1)S(1)}, u32[]{:S(2)}, u32[]{:S(2)}) collective-permute-start(bf16[48,1152]{1,0:T(8,128)(2,1)S(1)} %get-tuple-element.23.refs_5_), channel_id=1, source_target_pairs={{0,24},{2,26},{4,28},{6,30},{8,16},{10,18},{12,20},{14,22},{16,8},... | collective-permute-start | bytes 331784 | tf_op jit(solution)/shard_map/ppermute | solution.py:227
  20.8 1.7 %collective-permute-start.6 = (bf16[48,1152]{1,0:T(8,128)(2,1)S(1)}, bf16[48,1152]{1,0:T(8,128)(2,1)S(1)}, u32[]{:S(2)}, u32[]{:S(2)}) collective-permute-start(bf16[48,1152]{1,0:T(8,128)(2,1)S(1)} %get-tuple-element.23.refs_5_), channel_id=1, source_target_pairs={{0,16},{2,18},{4,20},{6,22},{8,24},{10,26},{12,28},{14,30},{16,0},... | collective-permute-start | bytes 331784 | tf_op jit(solution)/shard_map/ppermute | solution.py:227
  22.5 4.5 %collective-permute-done.7.refs_8_ = bf16[48,1152]{1,0:T(8,128)(2,1)S(1)} collective-permute-done((bf16[48,1152]{1,0:T(8,128)(2,1)S(1)}, bf16[48,1152]{1,0:T(8,128)(2,1)S(1)}, u32[]{:S(2)}, u32[]{:S(2)}) %collective-permute-start.7) | collective-permute-done | bytes 110624 | tf_op jit(solution)/shard_map/ppermute | solution.py:227
  26.9 2.6 %collective-permute-done.6.refs_7_ = bf16[48,1152]{1,0:T(8,128)(2,1)S(1)} collective-permute-done((bf16[48,1152]{1,0:T(8,128)(2,1)S(1)}, bf16[48,1152]{1,0:T(8,128)(2,1)S(1)}, u32[]{:S(2)}, u32[]{:S(2)}) %collective-permute-start.6) | collective-permute-done | bytes 110624 | tf_op jit(solution)/shard_map/ppermute | solution.py:227
  29.5 0.0 collective-permute-done.5.refs_6_
  29.5 0.0 copy-done.2
  29.5 0.0 copy-done.4
  29.5 0.6 %shard_map.67 = (f32[2,352,128]{2,1,0:T(8,128)S(1)}, f32[2,352,128]{2,1,0:T(8,128)S(1)}) custom-call(bf16[48,1024]{1,0:T(8,128)(2,1)S(1)} %copy-done.2, bf16[48,384]{1,0:T(8,128)(2,1)S(1)} %copy-done.4, bf16[48,1408]{1,0:T(8,128)(2,1)S(1)} %collective-permute-done.refs_0_.refs_2_, bf16[48,1408]{1,0:T(8,128)(2,1)S(1)} %collective-permute-done.1.refs_3_, ...), custom_call_target="tpu_custom_call" | custom-call | flops 1 | bytes 1 | tf_op jit(solution)/shard_map/pallas_call | solution.py:194
  30.2 0.1 collective-permute-start.8
  30.2 1.7 %collective-permute-done.8 = f32[2,352,128]{2,1,0:T(8,128)S(1)} collective-permute-done((f32[2,352,128]{2,1,0:T(8,128)S(1)}, f32[2,352,128]{2,1,0:T(8,128)S(1)}, u32[]{:S(2)}, u32[]{:S(2)}) %collective-permute-start.8) | collective-permute-done | bytes 360480 | tf_op jit(solution)/shard_map/ppermute | solution.py:284
  31.9 0.1 add.6
  32.0 1.6 %collective-permute-start.9 = (f32[1,352,128]{2,1,0:T(8,128)S(1)}, f32[1,352,128]{2,1,0:T(8,128)S(1)}, u32[]{:S(2)}, u32[]{:S(2)}) collective-permute-start(f32[1,352,128]{2,1,0:T(8,128)S(1)} %slice.9), channel_id=1, source_target_pairs={{0,4},{2,6},{4,0},{6,2},{8,12},{10,14},{12,8},{14,10},{16,20},{18,... | collective-permute-start | bytes 540680 | tf_op jit(solution)/shard_map/ppermute | solution.py:284
  33.5 5.1 %collective-permute-done.9 = f32[1,352,128]{2,1,0:T(8,128)S(1)} collective-permute-done((f32[1,352,128]{2,1,0:T(8,128)S(1)}, f32[1,352,128]{2,1,0:T(8,128)S(1)}, u32[]{:S(2)}, u32[]{:S(2)}) %collective-permute-start.9) | collective-permute-done | bytes 180256 | tf_op jit(solution)/shard_map/ppermute | solution.py:284
  38.6 0.7 %slice_add_fusion = f32[1,352,128]{2,1,0:T(8,128)} fusion(f32[1,352,128]{2,1,0:T(8,128)S(1)} %collective-permute-done.9, f32[2,352,128]{2,1,0:T(8,128)S(1)} %add.6), kind=kLoop, calls=%fused_computation | loop fusion | flops 45056 | bytes 540672 | tf_op jit(solution)/shard_map/add | solution.py:284
  (1 shorter events, 0.0 us)
Async XLA Ops:
  0.0 13.2 %copy-start = (bf16[1,1,2,48,704]{4,3,2,1,0:T(8,128)(2,1)S(1)}, bf16[1,1,2,48,704]{4,3,2,1,0:T(8,128)(2,1)}, u32[]{:S(2)}) copy-start(bf16[1,1,2,48,704]{4,3,2,1,0:T(8,128)(2,1)} %param.11) | copy-start | bytes 405508
  2.5 16.2 %collective-permute-start = (bf16[48,1408]{1,0:T(8,128)(2,1)}, bf16[48,1408]{1,0:T(8,128)(2,1)S(1)}, u32[]{:S(2)}, u32[]{:S(2)}) collective-permute-start(bf16[48,1408]{1,0:T(8,128)(2,1)} %get-tuple-element.18), channel_id=1, source_target_pairs={{0,8},{2,10},{4,12},{6,14},{8,0},{10,2},{12,4},{14,6},{16,24},{18,... | collective-permute-start | bytes 405512 | tf_op jit(solution)/shard_map/ppermute | solution.py:227
  5.6 13.2 %collective-permute-start.1 = (bf16[48,1408]{1,0:T(8,128)(2,1)}, bf16[48,1408]{1,0:T(8,128)(2,1)S(1)}, u32[]{:S(2)}, u32[]{:S(2)}) collective-permute-start(bf16[48,1408]{1,0:T(8,128)(2,1)} %get-tuple-element.19), channel_id=1, source_target_pairs={{0,16},{2,18},{4,20},{6,22},{8,24},{10,26},{12,28},{14,30},{16,0},... | collective-permute-start | bytes 405512 | tf_op jit(solution)/shard_map/ppermute | solution.py:227
  8.2 5.0 %collective-permute-start.3 = (bf16[48,1152]{1,0:T(8,128)(2,1)}, bf16[48,1152]{1,0:T(8,128)(2,1)S(1)}, u32[]{:S(2)}, u32[]{:S(2)}) collective-permute-start(bf16[48,1152]{1,0:T(8,128)(2,1)} %get-tuple-element.22), channel_id=1, source_target_pairs={{0,1},{1,0},{2,3},{3,2},{4,5},{5,4},{6,7},{7,6},{8,9},{9,8},{10,11... | collective-permute-start | bytes 331784 | tf_op jit(solution)/shard_map/ppermute | solution.py:222
  9.7 7.0 %collective-permute-start.2 = (bf16[48,384]{1,0:T(8,128)(2,1)}, bf16[48,384]{1,0:T(8,128)(2,1)S(1)}, u32[]{:S(2)}, u32[]{:S(2)}) collective-permute-start(bf16[48,384]{1,0:T(8,128)(2,1)} %get-tuple-element.20), channel_id=1, source_target_pairs={{0,24},{2,26},{4,28},{6,30},{8,16},{10,18},{12,20},{14,22},{16,8},... | collective-permute-start | bytes 110600 | tf_op jit(solution)/shard_map/ppermute | solution.py:227
  13.2 0.9 %copy-start.1 = (bf16[48,1024]{1,0:T(8,128)(2,1)S(1)}, bf16[48,1024]{1,0:T(8,128)(2,1)}, u32[]{:S(2)}) copy-start(bf16[48,1024]{1,0:T(8,128)(2,1)} %get-tuple-element.16.refs_1_.refs_0_) | copy-start | bytes 294916
  14.1 0.7 %copy-start.3 = (f32[48,128]{1,0:T(8,128)S(1)}, f32[48,128]{1,0:T(8,128)}, u32[]{:S(2)}) copy-start(f32[48,128]{1,0:T(8,128)} %get-tuple-element.21.refs_2_) | copy-start | bytes 73732
  15.1 14.4 %copy-start.2 = (bf16[48,1024]{1,0:T(8,128)(2,1)S(1)}, bf16[48,1024]{1,0:T(8,128)(2,1)}, u32[]{:S(2)}) copy-start(bf16[48,1024]{1,0:T(8,128)(2,1)} %get-tuple-element.16.refs_1_.refs_0_) | copy-start | bytes 294916
  15.2 14.4 %copy-start.4 = (bf16[48,384]{1,0:T(8,128)(2,1)S(1)}, bf16[48,384]{1,0:T(8,128)(2,1)}, u32[]{:S(2)}) copy-start(bf16[48,384]{1,0:T(8,128)(2,1)} %get-tuple-element.17.refs_1_) | copy-start | bytes 110596
  15.2 3.6 %collective-permute-start.4 = (f32[1,128]{1,0:T(1,128)S(1)}, f32[1,128]{1,0:T(1,128)S(1)}, u32[]{:S(2)}, u32[]{:S(2)}) collective-permute-start(f32[1,128]{1,0:T(1,128)S(1)} %shard_map.65.refs_5_), channel_id=1, source_target_pairs={{0,1},{1,0},{2,3},{3,2},{4,5},{5,4},{6,7},{7,6},{8,9},{9,8},{10,11... | collective-permute-start | bytes 1544 | tf_op jit(solution)/shard_map/ppermute | solution.py:222
  18.9 10.6 %collective-permute-start.5 = (bf16[48,2176]{1,0:T(8,128)(2,1)S(1)}, bf16[48,2176]{1,0:T(8,128)(2,1)S(1)}, u32[]{:S(2)}, u32[]{:S(2)}) collective-permute-start(bf16[48,2176]{1,0:T(8,128)(2,1)S(1)} %get-tuple-element.24), channel_id=1, source_target_pairs={{0,8},{2,10},{4,12},{6,14},{8,0},{10,2},{12,4},{14,6},{16,24},{18,... | collective-permute-start | bytes 626696 | tf_op jit(solution)/shard_map/ppermute | solution.py:227
  19.4 7.5 %collective-permute-start.7 = (bf16[48,1152]{1,0:T(8,128)(2,1)S(1)}, bf16[48,1152]{1,0:T(8,128)(2,1)S(1)}, u32[]{:S(2)}, u32[]{:S(2)}) collective-permute-start(bf16[48,1152]{1,0:T(8,128)(2,1)S(1)} %get-tuple-element.23.refs_5_), channel_id=1, source_target_pairs={{0,24},{2,26},{4,28},{6,30},{8,16},{10,18},{12,20},{14,22},{16,8},... | collective-permute-start | bytes 331784 | tf_op jit(solution)/shard_map/ppermute | solution.py:227
  20.8 8.7 %collective-permute-start.6 = (bf16[48,1152]{1,0:T(8,128)(2,1)S(1)}, bf16[48,1152]{1,0:T(8,128)(2,1)S(1)}, u32[]{:S(2)}, u32[]{:S(2)}) collective-permute-start(bf16[48,1152]{1,0:T(8,128)(2,1)S(1)} %get-tuple-element.23.refs_5_), channel_id=1, source_target_pairs={{0,16},{2,18},{4,20},{6,22},{8,24},{10,26},{12,28},{14,30},{16,0},... | collective-permute-start | bytes 331784 | tf_op jit(solution)/shard_map/ppermute | solution.py:227
  30.2 1.7 %collective-permute-start.8 = (f32[2,352,128]{2,1,0:T(8,128)S(1)}, f32[2,352,128]{2,1,0:T(8,128)S(1)}, u32[]{:S(2)}, u32[]{:S(2)}) collective-permute-start(f32[2,352,128]{2,1,0:T(8,128)S(1)} %get-tuple-element.26), channel_id=1, source_target_pairs={{0,2},{2,0},{4,6},{6,4},{8,10},{10,8},{12,14},{14,12},{16,18},{18,... | collective-permute-start | bytes 1081352 | tf_op jit(solution)/shard_map/ppermute | solution.py:284
  32.0 6.7 %collective-permute-start.9 = (f32[1,352,128]{2,1,0:T(8,128)S(1)}, f32[1,352,128]{2,1,0:T(8,128)S(1)}, u32[]{:S(2)}, u32[]{:S(2)}) collective-permute-start(f32[1,352,128]{2,1,0:T(8,128)S(1)} %slice.9), channel_id=1, source_target_pairs={{0,4},{2,6},{4,0},{6,2},{8,12},{10,14},{12,8},{14,10},{16,20},{18,... | collective-permute-start | bytes 540680 | tf_op jit(solution)/shard_map/ppermute | solution.py:284

commit v5 on v4

v5 whole, which is shorter than its diff:
```python
import jax
import jax.numpy as jnp
from jax import lax
from jax.experimental import pallas as pl
from jax.experimental.pallas import tpu as pltpu
from jax.sharding import PartitionSpec as P

EXAMPLES = 8
MATES = 4
LANES = 128
BF16 = jnp.bfloat16
F32 = jnp.float32


def iota(shape, axis):
    return lax.broadcasted_iota(jnp.int32, shape, axis)


def build(sources, cap, n_dp, pad, routes_at, weights_at, ids_at, loss_at, grad_at, hidden_at, *refs):
    own, own_code, *gives = refs[: sources + 1]
    parcels = refs[sources + 1 : sources + 1 + MATES]
    routes, weights, ids, loss, grad, hidden, sems = refs[sources + 1 + MATES :]
    fetches = [
        pltpu.make_async_copy(source, target, sems.at[i])
        for i, (source, target) in enumerate(
            [
                (routes_at, routes),
                (ids_at, ids),
                (loss_at, loss),
                (weights_at, weights),
                (hidden_at, hidden),
                (grad_at, grad),
            ]
        )
    ]
    for fetch in fetches:
        fetch.start()
    me = lax.axis_index("expert")
    tokens, width = grad.shape
    before = (iota((tokens, tokens), 0) < iota((tokens, tokens), 1)).astype(F32).astype(BF16)
    slot = iota((cap, tokens), 0).astype(F32)
    fetches[0].wait()
    matches = [routes[...] == lax.rem(me + (sources - k), sources) for k in range(sources)]
    hits = [jnp.sum(jnp.where(m, 1.0, 0.0), axis=0, keepdims=True) for m in matches]
    blank = -(-sources // 8) * 8 - sources
    routed = jnp.concatenate(hits + [jnp.zeros((1, tokens), F32)] * blank, axis=0)
    ranking = jnp.dot(routed.astype(BF16), before, preferred_element_type=F32)
    for fetch in fetches[1:4]:
        fetch.wait()
    token_ids = ids[...]
    token_weight = jnp.zeros((1, tokens), F32)
    for x in range(EXAMPLES):
        token_weight = jnp.where(token_ids == x, loss[0, x], token_weight)
    token_code = (token_ids + 1).astype(F32)
    ready = []
    for k in range(sources):
        scale = jnp.sum(jnp.where(matches[k], weights[...], 0.0), axis=0, keepdims=True)
        scale = scale * token_weight
        placed = jnp.where(ranking[k : k + 1] == slot, hits[k], 0.0)
        slot_scale = jnp.sum(placed * scale, axis=1, keepdims=True)
        code = jnp.sum(placed * token_code, axis=1, keepdims=True)
        ready.append((placed.astype(BF16), slot_scale, code))
    fetches[4].wait()
    cut_hidden(sources, n_dp, pad, width, hidden, parcels)
    fetches[5].wait()
    for k in range(sources):
        placed, slot_scale, code = ready[k]
        rows = jnp.dot(placed, grad[...], preferred_element_type=F32)
        rows = (rows * slot_scale).astype(BF16)
        if k == 0:
            own[...] = rows
            own_code[...] = jnp.broadcast_to(code, (cap, LANES))
            for parcel in parcels[1:]:
                parcel[:, :width] = rows
        else:
            gives[k - 1][:, :width] = rows
            gives[k - 1][:, width:] = jnp.broadcast_to(code, (cap, LANES)).astype(BF16)


def cut_hidden(sources, n_dp, pad, width, hidden, parcels):
    me, rank = lax.axis_index("expert"), lax.axis_index("dp")
    spread = n_dp // MATES
    cap, ff = hidden.shape[1:]
    rows = ff // n_dp
    high, low = rank // MATES, lax.rem(rank, MATES)
    column = iota((1, spread * pad), 1)
    wanted = jnp.full((1, spread * pad), -2 * ff, jnp.int32)
    for p in range(spread):
        inside = (column >= p * pad) & (column < p * pad + rows)
        wanted = jnp.where(inside, (high ^ p) * (MATES * rows) + column - p * pad, wanted)
    unit = iota((ff, spread * pad), 0)
    acts = [hidden[lax.rem(me + j, sources)] for j in range(sources)]
    acts = jnp.concatenate(acts, axis=0)
    for k in range(MATES):
        pick = jnp.where(unit == wanted + (low ^ k) * rows, 1.0, 0.0).astype(BF16)
        units = jnp.dot(acts, pick, preferred_element_type=F32).astype(BF16)
        first = width if k else 0
        for j in range(sources):
            at = slice(first + j * spread * pad, first + (j + 1) * spread * pad)
            parcels[k][:, at] = units[j * cap : (j + 1) * cap]


def stage(sources, own_at, code_at, hidden_at, own, own_code, left, hidden, sems):
    fetches = [
        pltpu.make_async_copy(source, target, sems.at[i])
        for i, (source, target) in enumerate(
            [(hidden_at, hidden), (own_at, own), (code_at, own_code)]
        )
    ]
    for fetch in fetches:
        fetch.start()
    me = lax.axis_index("expert")
    fetches[0].wait()
    acts = jnp.concatenate([hidden[lax.rem(me + j, sources)] for j in range(sources)], axis=0)
    left[...] = lax.dot_general(
        acts, acts, (((1,), (1,)), ((), ())), preferred_element_type=F32
    )
    fetches[1].wait()
    fetches[2].wait()


def norms(sources, left, own, own_code, *refs):
    takes, squares = refs[: sources - 1], refs[sources - 1]
    width = own.shape[1]
    cot = jnp.concatenate([own[...]] + [t[:, :width] for t in takes], axis=0)
    member = membership(own_code, takes, width)
    last = (((1,), (1,)), ((), ()))
    right = lax.dot_general(cot, cot, last, preferred_element_type=F32)
    one_hot = member.astype(BF16)
    alike = lax.dot_general(one_hot, one_hot, last, preferred_element_type=F32)
    per_slot = jnp.sum(left[...] * right * alike, axis=1, keepdims=True)
    squares[...] = jnp.sum(per_slot * member, axis=0, keepdims=True)


def membership(own_code, takes, width):
    code = jnp.concatenate(
        [own_code[...]] + [t[:, width:].astype(F32) for t in takes], axis=0
    )
    lane = iota(code.shape, 1).astype(F32)
    return jnp.where((code == lane) & (code > 0.0), 1.0, 0.0)


def scale(sources, count, own_code, *refs):
    takes, squares, rest = refs[: sources - 1], refs[sources - 1 : -1], refs[-1]
    cap = own_code.shape[0]
    width = takes[0].shape[1] - LANES
    total = squares[0][...]
    for s in squares[1:]:
        total = total + s[...]
    clip = 1.0 / jnp.maximum(jnp.sqrt(total / count), 1.0)
    member = membership(own_code, takes, width)
    weight = jnp.sum(member * clip, axis=1, keepdims=True) / EXAMPLES
    own_weight = jnp.broadcast_to(weight[:cap], (cap, LANES))
    high = own_weight.astype(BF16).astype(F32)
    middle = (own_weight - high).astype(BF16).astype(F32)
    low = own_weight - high - middle
    lane = iota((cap, LANES), 1)
    three = jnp.where(lane == 0, high, jnp.where(lane == 1, middle, low)).astype(BF16)
    for j in range(1, sources):
        part = slice((j - 1) * cap, j * cap)
        slot_weight = weight[j * cap : (j + 1) * cap]
        rows = slot_weight * takes[j - 1][:, :width].astype(F32)
        rest[part, :width] = rows.astype(BF16)
        rest[part, width:] = three


def product(sources, rows, pad, *refs):
    own, cut, *parcels = refs[: MATES + 1]
    rests = refs[MATES + 1 : 2 * MATES + 1]
    keep, *leave, cots, units = refs[2 * MATES + 1 :]
    cap, width = own.shape
    across = units.shape[1]
    slots = sources * cap
    owns = [own] + [parcel.at[:, :width] for parcel in parcels]
    cuts = [cut] + [parcel.at[:, width:] for parcel in parcels]
    for k in range(MATES):
        three = rests[k][:cap, width:].astype(F32)
        weight = three[:, 0:1] + three[:, 1:2] + three[:, 2:3]
        at = k * slots
        cots[at : at + cap] = (weight * owns[k][...].astype(F32)).astype(BF16)
        cots[at + cap : at + slots] = rests[k][:, :width]
        for j in range(sources):
            units[at + j * cap : at + (j + 1) * cap] = cuts[k][:, j * across : (j + 1) * across]
    pieces = width // LANES
    part = lax.dot_general(
        units[...], cots[...], (((0,), (0,)), ((), ())), preferred_element_type=F32
    )
    for p, out in enumerate([keep] + leave):
        values = part[p * pad : p * pad + rows]
        if p:
            most = jnp.max(jnp.max(jnp.abs(values), axis=0, keepdims=True), axis=1, keepdims=True)
            exponent = jnp.ceil(jnp.log2(jnp.maximum(most, 2.0**-100)))
            values = values * jnp.exp2(-exponent)
            below = out.shape[0] - rows * pieces
            out[rows * pieces :] = jnp.broadcast_to(exponent, (below, LANES))
        for j in range(pieces):
            out[pl.ds(j, rows, stride=pieces), :] = values[:, j * LANES : (j + 1) * LANES]


def call(body, outs, args, fetched=(), scratch=(), limit=32, flops=1):
    vmem = pl.BlockSpec(memory_space=pltpu.VMEM)
    anywhere = pl.BlockSpec(memory_space=pl.ANY)
    return pl.pallas_call(
        body,
        out_shape=tuple(outs),
        in_specs=[anywhere if i in fetched else vmem for i in range(len(args))],
        out_specs=tuple([vmem] * len(outs)),
        scratch_shapes=list(scratch),
        compiler_params=pltpu.CompilerParams(vmem_limit_bytes=limit * 1024 * 1024),
        cost_estimate=pl.CostEstimate(flops=flops, bytes_accessed=1, transcendentals=0),
    )(*args)


def shards(grad_out, routes, route_weight, example_ids, example_weight, hidden):
    sources = lax.axis_size("expert")
    n_dp = lax.axis_size("dp")
    spread = n_dp // MATES
    tokens, width = grad_out.shape
    top = routes.shape[1]
    cap, ff = hidden.shape[3], hidden.shape[4]
    rows = ff // n_dp
    pad = -(-rows // 16) * 16
    while spread * pad * sources % LANES:
        pad += 16
    across = spread * pad
    slots = sources * cap
    acts = hidden.reshape(sources, cap, ff)
    shape = jax.ShapeDtypeStruct

    def over_experts(array, k):
        return lax.ppermute(
            array, "expert", [(s, (s - k) % sources) for s in range(sources)]
        )

    def over_dp(array, k):
        return lax.ppermute(array, "dp", [(i, i ^ k) for i in range(n_dp)])

    own_made, code_made, *made = call(
        lambda *refs: build(sources, cap, n_dp, pad, *refs),
        [shape((cap, width), BF16), shape((cap, LANES), F32)]
        + [shape((cap, width + LANES), BF16)] * (sources - 1)
        + [
            shape((cap, sources * across + (width if k else 0)), BF16) for k in range(MATES)
        ],
        (routes.T, route_weight.T, example_ids, example_weight, grad_out, acts),
        fetched=range(6),
        limit=60,
        scratch=(
            pltpu.VMEM((top, tokens), jnp.int32),
            pltpu.VMEM((top, tokens), F32),
            pltpu.VMEM((1, tokens), jnp.int32),
            pltpu.SMEM((1, EXAMPLES), F32),
            pltpu.VMEM((tokens, width), BF16),
            pltpu.VMEM((sources, cap, ff), BF16),
            pltpu.SemaphoreType.DMA((6,)),
        ),
    )
    gives, (cut, *parcels) = made[: sources - 1], made[sources - 1 :]
    takes = [over_experts(g, k + 1) for k, g in enumerate(gives)]
    parcels = [over_dp(parcel, k + 1) for k, parcel in enumerate(parcels)]
    own, own_code, left = call(
        lambda *refs: stage(sources, *refs),
        [shape((cap, width), BF16), shape((cap, LANES), F32), shape((slots, slots), F32)],
        (own_made, code_made, acts),
        fetched=range(3),
        scratch=(pltpu.VMEM((sources, cap, ff), BF16), pltpu.SemaphoreType.DMA((3,))),
        flops=1 << 32,
    )
    (squares,) = call(
        lambda *refs: norms(sources, *refs),
        [shape((1, LANES), F32)],
        (left, own, own_code, *takes),
        flops=1 << 32,
    )
    all_squares = [squares] + [over_experts(squares, k) for k in range(1, sources)]
    (rest,) = call(
        lambda *refs: scale(sources, ff * width, *refs),
        [shape((slots - cap, width + LANES), BF16)],
        (own_code, *takes, *all_squares),
    )
    rests = [rest] + [over_dp(rest, k) for k in range(1, MATES)]

    held = rows * (width // LANES)
    sent = -(-(held + 8) // 16) * 16
    part, *leave = call(
        lambda *refs: product(sources, rows, pad, *refs),
        [shape((held if p == 0 else sent, LANES), F32) for p in range(spread)],
        (own, cut, *parcels, *rests),
        scratch=(
            pltpu.VMEM((MATES * slots, width), BF16),
            pltpu.VMEM((MATES * slots, across), BF16),
        ),
    )
    for p in range(1, spread):
        got = over_dp(leave[p - 1].astype(jnp.float16), p * MATES).astype(F32)
        part = part + got[:held] * jnp.exp2(got[held : held + 1])
    return part.reshape(rows, 1, width)


def solution(mesh):
    placed = (
        P(("dp", "expert"), None),
        P(("dp", "expert"), None),
        P(("dp", "expert"), None),
        P("dp", "expert"),
        P("dp", None),
        P("dp", "expert", None, None, None),
    )
    return jax.shard_map(
        shards, mesh=mesh, in_specs=placed, out_specs=P("dp", "expert", None), check_vma=False
    )
```

time: 39.5 us -> 35.2 us (0.89)
  waiting for transfers between devices: 19.1 us -> 15.7 us
  starting transfers between devices: 14.2 us -> 12.3 us
  Pallas kernels: 3.61 us -> 4.3 us
    ppermute x8 -> x9, starting transfers between devices: 11.1 us -> 8.3 us  [over_dp(): return lax.ppermute(array, 'dp', [(i, i ^ k) for i in range(n_dp)])]
    ppermute x2, waiting for transfers between devices: 5.24 us -> 2.59 us  [over_experts(): lax.ppermute(array, 'expert', [(s, (s - k) % sources) for s in range(sour...]
    ppermute x2, starting transfers between devices: 3.1 us -> 4.05 us  [over_experts(): lax.ppermute(array, 'expert', [(s, (s - k) % sources) for s in range(sour...]
    ppermute x8 -> x9, waiting for transfers between devices: 13.8 us -> 13.1 us  [over_dp(): return lax.ppermute(array, 'dp', [(i, i ^ k) for i in range(n_dp)])]
    pallas_call x4 -> x5, Pallas kernels: 3.61 us -> 4.3 us  [call(): pl.pallas_call(body, out_shape=tuple(outs), in_specs=[anywhere if i in fe...]
    unnamed x10 -> x8, local copies, waits for them, and re-layouts: 1.64 us -> 1.64 us
  transfers between devices with their start and end apart: 10 -> 11, of which waited for: 6 -> 5; matrix products, arithmetic and copies ran while one was open for 0% -> 0% of each run, Pallas kernels for 1% -> 3%
where the time goes in v5:
time: 35.2 us; the launch traced here: 34.9 us
  waiting for transfers between devices  15.7 us (45%)
  starting transfers between devices  12.3 us (35%)
  Pallas kernels  4.3 us (12%)
  local copies, waits for them, and re-layouts  1.64 us (5%)
  other arithmetic  0.84 us (2%)
    ppermute x9, waiting for transfers between devices, over_dp(): return lax.ppermute(array, 'dp', [(i, i ^ k) for i in range(n_dp)])  13.1 us
    ppermute x9, starting transfers between devices, over_dp(): return lax.ppermute(array, 'dp', [(i, i ^ k) for i in range(n_dp)])  8.3 us
    pallas_call x5, Pallas kernels, call(): pl.pallas_call(body, out_shape=tuple(outs), in_specs=[anywhere if i in fe...  4.3 us
    ppermute x2, starting transfers between devices, over_experts(): lax.ppermute(array, 'expert', [(s, (s - k) % sources) for s in range(sour...  4.05 us
    ppermute x2, waiting for transfers between devices, over_experts(): lax.ppermute(array, 'expert', [(s, (s - k) % sources) for s in range(sour...  2.59 us
    unnamed x8, local copies, waits for them, and re-layouts  1.64 us
    add x1, other arithmetic, shards(): part = part + got[:held] * jnp.exp2(got[held:held + 1])  0.73 us
  transfers between devices with their start and end apart: 11, of which 5 were waited for; matrix products, arithmetic and copies ran while one was open for 0% of the time, Pallas kernels for 3%

profile of v5, /device:TPU:0, one launch (start us, length us, event | category | flops | bytes accessed | tf_op | source)
XLA Modules:
  0.0 34.9 jit_solution(505640775916991745)
XLA Ops:
  0.0 0.0 copy-start
  0.0 2.5 %shard_map.64 = (bf16[48,1024]{1,0:T(8,128)(2,1)}, f32[48,128]{1,0:T(8,128)}, bf16[48,1152]{1,0:T(8,128)(2,1)}, bf16[48,384]{1,0:T(8,128)(2,1)}, bf16[48,1408]{1...) custom-call(s32[6,256]{1,0:T(8,128)} %bitcast.12, f32[6,256]{1,0:T(8,128)} %bitcast.13, ...), custom_call_target="tpu_custom_call" | custom-call | flops 1 | bytes 1 | tf_op jit(solution)/shard_map/pallas_call | solution.py:203
  2.6 3.0 %collective-permute-start.3 = (bf16[48,1152]{1,0:T(8,128)(2,1)}, bf16[48,1152]{1,0:T(8,128)(2,1)S(1)}, u32[]{:S(2)}, u32[]{:S(2)}) collective-permute-start(bf16[48,1152]{1,0:T(8,128)(2,1)} %get-tuple-element.27), channel_id=1, source_target_pairs={{0,1},{1,0},{2,3},{3,2},{4,5},{5,4},{6,7},{7,6},{8,9},{9,8},{10,11... | collective-permute-start | bytes 331784 | tf_op jit(solution)/shard_map/ppermute | solution.py:231
  5.6 0.0 collective-permute-start
  5.6 1.5 %collective-permute-start.1 = (bf16[48,1408]{1,0:T(8,128)(2,1)}, bf16[48,1408]{1,0:T(8,128)(2,1)S(1)}, u32[]{:S(2)}, u32[]{:S(2)}) collective-permute-start(bf16[48,1408]{1,0:T(8,128)(2,1)} %get-tuple-element.24), channel_id=1, source_target_pairs={{0,4},{2,6},{4,0},{6,2},{8,12},{10,14},{12,8},{14,10},{16,20},{18,... | collective-permute-start | bytes 405512 | tf_op jit(solution)/shard_map/ppermute | solution.py:236
  7.1 0.4 %collective-permute-start.2 = (bf16[48,1408]{1,0:T(8,128)(2,1)}, bf16[48,1408]{1,0:T(8,128)(2,1)S(1)}, u32[]{:S(2)}, u32[]{:S(2)}) collective-permute-start(bf16[48,1408]{1,0:T(8,128)(2,1)} %get-tuple-element.25), channel_id=1, source_target_pairs={{0,6},{2,4},{4,2},{6,0},{8,14},{10,12},{12,10},{14,8},{16,22},{18,... | collective-permute-start | bytes 405512 | tf_op jit(solution)/shard_map/ppermute | solution.py:236
  7.5 0.0 copy-done
  7.5 0.0 copy-start.2
  7.5 0.9 %copy-done.2 = bf16[48,1024]{1,0:T(8,128)(2,1)S(1)} copy-done((bf16[48,1024]{1,0:T(8,128)(2,1)S(1)}, bf16[48,1024]{1,0:T(8,128)(2,1)}, u32[]{:S(2)}) %copy-start.2) | copy-done | bytes 98328
  8.3 0.0 copy-start.3
  8.3 0.7 %copy-done.3 = f32[48,128]{1,0:T(8,128)S(1)} copy-done((f32[48,128]{1,0:T(8,128)S(1)}, f32[48,128]{1,0:T(8,128)}, u32[]{:S(2)}) %copy-start.3) | copy-done | bytes 24600
  9.1 0.5 %shard_map.65 = (bf16[48,1024]{1,0:T(8,128)(2,1)S(1)}, f32[48,128]{1,0:T(8,128)S(1)}, f32[96,96]{1,0:T(8,128)S(1)}) custom-call(bf16[48,1024]{1,0:T(8,128)(2,1)S(1)} %copy-done.2, f32[48,128]{1,0:T(8,128)S(1)} %copy-done.3, bf16[2,48,704]{2,1,0:T(8,128)(2,1)S(1)} %bitcast.11), custom_call_target="tpu_custom_call" | custom-call | flops 4294967296 | bytes 1 | tf_op jit(solution)/shard_map/pallas_call | solution.py:203
  9.6 0.0 collective-permute-done.3.refs_3_.refs_1_
  9.6 0.3 shard_map.66.refs_2_
  10.0 0.0 copy-start.1
  10.0 1.0 %collective-permute-start.4 = (f32[1,128]{1,0:T(1,128)S(1)}, f32[1,128]{1,0:T(1,128)S(1)}, u32[]{:S(2)}, u32[]{:S(2)}) collective-permute-start(f32[1,128]{1,0:T(1,128)S(1)} %shard_map.66.refs_2_), channel_id=1, source_target_pairs={{0,1},{1,0},{2,3},{3,2},{4,5},{5,4},{6,7},{7,6},{8,9},{9,8},{10,11... | collective-permute-start | bytes 1544 | tf_op jit(solution)/shard_map/ppermute | solution.py:231
  11.0 2.6 %collective-permute-done.4.refs_3_ = f32[1,128]{1,0:T(1,128)S(1)} collective-permute-done((f32[1,128]{1,0:T(1,128)S(1)}, f32[1,128]{1,0:T(1,128)S(1)}, u32[]{:S(2)}, u32[]{:S(2)}) %collective-permute-start.4) | collective-permute-done | bytes 544 | tf_op jit(solution)/shard_map/ppermute | solution.py:231
  13.6 0.1 shard_map.67.refs_5_
  13.7 0.6 %collective-permute-start.7 = (bf16[48,1152]{1,0:T(8,128)(2,1)S(1)}, bf16[48,1152]{1,0:T(8,128)(2,1)S(1)}, u32[]{:S(2)}, u32[]{:S(2)}) collective-permute-start(bf16[48,1152]{1,0:T(8,128)(2,1)S(1)} %shard_map.67.refs_5_), channel_id=1, source_target_pairs={{0,6},{2,4},{4,2},{6,0},{8,14},{10,12},{12,10},{14,8},{16,22},{18,... | collective-permute-start | bytes 331784 | tf_op jit(solution)/shard_map/ppermute | solution.py:236
  14.3 1.0 %collective-permute-start.6 = (bf16[48,1152]{1,0:T(8,128)(2,1)S(1)}, bf16[48,1152]{1,0:T(8,128)(2,1)S(1)}, u32[]{:S(2)}, u32[]{:S(2)}) collective-permute-start(bf16[48,1152]{1,0:T(8,128)(2,1)S(1)} %shard_map.67.refs_5_), channel_id=1, source_target_pairs={{0,4},{2,6},{4,0},{6,2},{8,12},{10,14},{12,8},{14,10},{16,20},{18,... | collective-permute-start | bytes 331784 | tf_op jit(solution)/shard_map/ppermute | solution.py:236
  15.3 0.0 collective-permute-done.refs_2_
  15.3 0.3 collective-permute-start.5
  15.6 0.0 collective-permute-done.1.refs_3_
  15.6 0.0 collective-permute-done.2.refs_4_
  15.6 3.4 %collective-permute-done.7.refs_8_ = bf16[48,1152]{1,0:T(8,128)(2,1)S(1)} collective-permute-done((bf16[48,1152]{1,0:T(8,128)(2,1)S(1)}, bf16[48,1152]{1,0:T(8,128)(2,1)S(1)}, u32[]{:S(2)}, u32[]{:S(2)}) %collective-permute-start.7) | collective-permute-done | bytes 110624 | tf_op jit(solution)/shard_map/ppermute | solution.py:236
  19.1 2.4 %collective-permute-done.6.refs_7_ = bf16[48,1152]{1,0:T(8,128)(2,1)S(1)} collective-permute-done((bf16[48,1152]{1,0:T(8,128)(2,1)S(1)}, bf16[48,1152]{1,0:T(8,128)(2,1)S(1)}, u32[]{:S(2)}, u32[]{:S(2)}) %collective-permute-start.6) | collective-permute-done | bytes 110624 | tf_op jit(solution)/shard_map/ppermute | solution.py:236
  21.5 0.0 collective-permute-done.5.refs_6_
  21.5 0.0 copy-done.1
  21.5 0.8 %shard_map.68 = (f32[352,128]{1,0:T(8,128)S(1)}, f32[368,128]{1,0:T(8,128)S(1)}, f32[368,128]{1,0:T(8,128)S(1)}, f32[368,128]{1,0:T(8,128)S(1)}) custom-call(bf16[48,1024]{1,0:T(8,128)(2,1)S(1)} %get-tuple-element.21.refs_1_.refs_0_, bf16[48,384]{1,0:T(8,128)(2,1)S(1)} %copy-done.1, bf16[48,1408]{1,0:T(8,128)(2,1)S(1)} %collective-permute-done.refs_2_, ...), custom_call_target="tpu_custom_call" | custom-call | flops 1 | bytes 1 | tf_op jit(solution)/shard_map/pallas_call | solution.py:203
  22.3 3.7 %collective-permute-start.10 = (f16[368,128]{1,0:T(8,128)(2,1)S(1)}, f16[368,128]{1,0:T(8,128)(2,1)S(1)}, u32[]{:S(2)}, u32[]{:S(2)}) collective-permute-start(f16[368,128]{1,0:T(8,128)(2,1)S(1)} %convert_element_type.22), channel_id=1, source_target_pairs={{0,24},{2,26},{4,28},{6,30},{8,16},{10,18},{12,20},{14,22},{16,8},... | collective-permute-start | bytes 282632 | tf_op jit(solution)/shard_map/ppermute | solution.py:236
  26.0 0.1 collective-permute-start.9
  26.1 0.8 %collective-permute-start.8 = (f16[368,128]{1,0:T(8,128)(2,1)S(1)}, f16[368,128]{1,0:T(8,128)(2,1)S(1)}, u32[]{:S(2)}, u32[]{:S(2)}) collective-permute-start(f16[368,128]{1,0:T(8,128)(2,1)S(1)} %convert_element_type.18), channel_id=1, source_target_pairs={{0,8},{2,10},{4,12},{6,14},{8,0},{10,2},{12,4},{14,6},{16,24},{18,... | collective-permute-start | bytes 282632 | tf_op jit(solution)/shard_map/ppermute | solution.py:236
  26.9 2.8 %collective-permute-done.10 = f16[368,128]{1,0:T(8,128)(2,1)S(1)} collective-permute-done((f16[368,128]{1,0:T(8,128)(2,1)S(1)}, f16[368,128]{1,0:T(8,128)(2,1)S(1)}, u32[]{:S(2)}, u32[]{:S(2)}) %collective-permute-start.10) | collective-permute-done | bytes 94240 | tf_op jit(solution)/shard_map/ppermute | solution.py:236
  29.7 4.4 %collective-permute-done.9 = f16[368,128]{1,0:T(8,128)(2,1)S(1)} collective-permute-done((f16[368,128]{1,0:T(8,128)(2,1)S(1)}, f16[368,128]{1,0:T(8,128)(2,1)S(1)}, u32[]{:S(2)}, u32[]{:S(2)}) %collective-permute-start.9) | collective-permute-done | bytes 94240 | tf_op jit(solution)/shard_map/ppermute | solution.py:236
  34.2 0.0 collective-permute-done.8
  34.2 0.7 %fusion = f32[352,128]{1,0:T(8,128)} fusion(f32[368,128]{1,0:T(8,128)S(1)} %convert_element_type.23, f32[368,128]{1,0:T(8,128)S(1)} %convert_element_type.21, f32[352,128]{1,0:T(8,128)S(1)} %get-tuple-element.29, f32[368,128]{1,0:T(8,128)S(1)} %convert_element_type.19, f32[128]{0:T(128)S(1)} %fusion.4, f32[128]{0:T(128)S(1)} %fusion.6, f32[128]{0:T(128)S(1)} %fusion.8), kind=kLoop, calls=%fused_computation.1 | loop fusion | flops 270336 | bytes 902656 | tf_op jit(solution)/shard_map/add | solution.py:296
  (9 shorter events, 0.1 us)
Async XLA Ops:
  0.0 7.5 %copy-start = (bf16[1,1,2,48,704]{4,3,2,1,0:T(8,128)(2,1)S(1)}, bf16[1,1,2,48,704]{4,3,2,1,0:T(8,128)(2,1)}, u32[]{:S(2)}) copy-start(bf16[1,1,2,48,704]{4,3,2,1,0:T(8,128)(2,1)} %param.11) | copy-start | bytes 405508
  2.6 7.1 %collective-permute-start.3 = (bf16[48,1152]{1,0:T(8,128)(2,1)}, bf16[48,1152]{1,0:T(8,128)(2,1)S(1)}, u32[]{:S(2)}, u32[]{:S(2)}) collective-permute-start(bf16[48,1152]{1,0:T(8,128)(2,1)} %get-tuple-element.27), channel_id=1, source_target_pairs={{0,1},{1,0},{2,3},{3,2},{4,5},{5,4},{6,7},{7,6},{8,9},{9,8},{10,11... | collective-permute-start | bytes 331784 | tf_op jit(solution)/shard_map/ppermute | solution.py:231
  5.6 9.8 %collective-permute-start = (bf16[48,1408]{1,0:T(8,128)(2,1)}, bf16[48,1408]{1,0:T(8,128)(2,1)S(1)}, u32[]{:S(2)}, u32[]{:S(2)}) collective-permute-start(bf16[48,1408]{1,0:T(8,128)(2,1)} %get-tuple-element.23), channel_id=1, source_target_pairs={{0,2},{2,0},{4,6},{6,4},{8,10},{10,8},{12,14},{14,12},{16,18},{18,... | collective-permute-start | bytes 405512 | tf_op jit(solution)/shard_map/ppermute | solution.py:236
  5.6 10.0 %collective-permute-start.1 = (bf16[48,1408]{1,0:T(8,128)(2,1)}, bf16[48,1408]{1,0:T(8,128)(2,1)S(1)}, u32[]{:S(2)}, u32[]{:S(2)}) collective-permute-start(bf16[48,1408]{1,0:T(8,128)(2,1)} %get-tuple-element.24), channel_id=1, source_target_pairs={{0,4},{2,6},{4,0},{6,2},{8,12},{10,14},{12,8},{14,10},{16,20},{18,... | collective-permute-start | bytes 405512 | tf_op jit(solution)/shard_map/ppermute | solution.py:236
  7.1 8.6 %collective-permute-start.2 = (bf16[48,1408]{1,0:T(8,128)(2,1)}, bf16[48,1408]{1,0:T(8,128)(2,1)S(1)}, u32[]{:S(2)}, u32[]{:S(2)}) collective-permute-start(bf16[48,1408]{1,0:T(8,128)(2,1)} %get-tuple-element.25), channel_id=1, source_target_pairs={{0,6},{2,4},{4,2},{6,0},{8,14},{10,12},{12,10},{14,8},{16,22},{18,... | collective-permute-start | bytes 405512 | tf_op jit(solution)/shard_map/ppermute | solution.py:236
  7.5 0.9 %copy-start.2 = (bf16[48,1024]{1,0:T(8,128)(2,1)S(1)}, bf16[48,1024]{1,0:T(8,128)(2,1)}, u32[]{:S(2)}) copy-start(bf16[48,1024]{1,0:T(8,128)(2,1)} %get-tuple-element.19.refs_0_) | copy-start | bytes 294916
  8.3 0.7 %copy-start.3 = (f32[48,128]{1,0:T(8,128)S(1)}, f32[48,128]{1,0:T(8,128)}, u32[]{:S(2)}) copy-start(f32[48,128]{1,0:T(8,128)} %get-tuple-element.20.refs_1_) | copy-start | bytes 73732
  10.0 11.5 %copy-start.1 = (bf16[48,384]{1,0:T(8,128)(2,1)S(1)}, bf16[48,384]{1,0:T(8,128)(2,1)}, u32[]{:S(2)}) copy-start(bf16[48,384]{1,0:T(8,128)(2,1)} %get-tuple-element.22.refs_1_) | copy-start | bytes 110596
  10.0 3.6 %collective-permute-start.4 = (f32[1,128]{1,0:T(1,128)S(1)}, f32[1,128]{1,0:T(1,128)S(1)}, u32[]{:S(2)}, u32[]{:S(2)}) collective-permute-start(f32[1,128]{1,0:T(1,128)S(1)} %shard_map.66.refs_2_), channel_id=1, source_target_pairs={{0,1},{1,0},{2,3},{3,2},{4,5},{5,4},{6,7},{7,6},{8,9},{9,8},{10,11... | collective-permute-start | bytes 1544 | tf_op jit(solution)/shard_map/ppermute | solution.py:231
  13.7 5.4 %collective-permute-start.7 = (bf16[48,1152]{1,0:T(8,128)(2,1)S(1)}, bf16[48,1152]{1,0:T(8,128)(2,1)S(1)}, u32[]{:S(2)}, u32[]{:S(2)}) collective-permute-start(bf16[48,1152]{1,0:T(8,128)(2,1)S(1)} %shard_map.67.refs_5_), channel_id=1, source_target_pairs={{0,6},{2,4},{4,2},{6,0},{8,14},{10,12},{12,10},{14,8},{16,22},{18,... | collective-permute-start | bytes 331784 | tf_op jit(solution)/shard_map/ppermute | solution.py:236
  14.3 7.2 %collective-permute-start.6 = (bf16[48,1152]{1,0:T(8,128)(2,1)S(1)}, bf16[48,1152]{1,0:T(8,128)(2,1)S(1)}, u32[]{:S(2)}, u32[]{:S(2)}) collective-permute-start(bf16[48,1152]{1,0:T(8,128)(2,1)S(1)} %shard_map.67.refs_5_), channel_id=1, source_target_pairs={{0,4},{2,6},{4,0},{6,2},{8,12},{10,14},{12,8},{14,10},{16,20},{18,... | collective-permute-start | bytes 331784 | tf_op jit(solution)/shard_map/ppermute | solution.py:236
  15.3 6.2 %collective-permute-start.5 = (bf16[48,1152]{1,0:T(8,128)(2,1)S(1)}, bf16[48,1152]{1,0:T(8,128)(2,1)S(1)}, u32[]{:S(2)}, u32[]{:S(2)}) collective-permute-start(bf16[48,1152]{1,0:T(8,128)(2,1)S(1)} %shard_map.67.refs_5_), channel_id=1, source_target_pairs={{0,2},{2,0},{4,6},{6,4},{8,10},{10,8},{12,14},{14,12},{16,18},{18,... | collective-permute-start | bytes 331784 | tf_op jit(solution)/shard_map/ppermute | solution.py:236
  22.3 7.4 %collective-permute-start.10 = (f16[368,128]{1,0:T(8,128)(2,1)S(1)}, f16[368,128]{1,0:T(8,128)(2,1)S(1)}, u32[]{:S(2)}, u32[]{:S(2)}) collective-permute-start(f16[368,128]{1,0:T(8,128)(2,1)S(1)} %convert_element_type.22), channel_id=1, source_target_pairs={{0,24},{2,26},{4,28},{6,30},{8,16},{10,18},{12,20},{14,22},{16,8},... | collective-permute-start | bytes 282632 | tf_op jit(solution)/shard_map/ppermute | solution.py:236
  26.0 8.1 %collective-permute-start.9 = (f16[368,128]{1,0:T(8,128)(2,1)S(1)}, f16[368,128]{1,0:T(8,128)(2,1)S(1)}, u32[]{:S(2)}, u32[]{:S(2)}) collective-permute-start(f16[368,128]{1,0:T(8,128)(2,1)S(1)} %convert_element_type.20), channel_id=1, source_target_pairs={{0,16},{2,18},{4,20},{6,22},{8,24},{10,26},{12,28},{14,30},{16,0},... | collective-permute-start | bytes 282632 | tf_op jit(solution)/shard_map/ppermute | solution.py:236
  26.1 8.1 %collective-permute-start.8 = (f16[368,128]{1,0:T(8,128)(2,1)S(1)}, f16[368,128]{1,0:T(8,128)(2,1)S(1)}, u32[]{:S(2)}, u32[]{:S(2)}) collective-permute-start(f16[368,128]{1,0:T(8,128)(2,1)S(1)} %convert_element_type.18), channel_id=1, source_target_pairs={{0,8},{2,10},{4,12},{6,14},{8,0},{10,2},{12,4},{14,6},{16,24},{18,... | collective-permute-start | bytes 282632 | tf_op jit(solution)/shard_map/ppermute | solution.py:236
